TPU v7x, 512 devices: a whole 4x4x16 slice. The times are simulated.
512 devices in a mesh: layer: 2 (over x_lo), row: 16 (over y, x_hi, core), col: 16 (over z).
Axes of the slice: x: 4 (x_hi: 2, x_lo: 2; x = x_hi * 2 + x_lo), y: 4, z: 16, core: 2. Of those that a mesh axis runs over, the one named last changes fastest.
Arguments:
- x_blocks: bfloat16 [16, 16, 32, 128, 128], P('col', 'row'), may hold values from -1.5 to 1.5
- x_coords: int32 [16, 16, 2, 32], P('col', 'row'), may hold values from -1 to 127, as said below
Outputs:
- c_blocks: float32 [16, 16, 32, 128, 128], P('col', 'row', 'layer')
Inputs may be any that keep to these rules, and one draw needn't show every extreme that they name: `x_coords`: each band b has one set of 8 block rows used in it: every non-empty slot of a tile (I, J) has its block row in the set of band I and its block column in the set of band J, and every tile uses all 8 rows of its set and all 8 columns of its set. No block appears twice in a tile. Non-empty slots come first; each tile has 8 to 32 of them, and some tile has 32.
All inputs are finite; a program needn't handle non-finite values.
Results may differ from a plain program's by a relative error of at most 0.0003.
Values may be sent and summed in bfloat16 or wider, within the bound.
No kernel may reach another device: no remote copies, remote signals or barrier semaphores. Data moves between devices by JAX's collectives and lax.ppermute only.
A program may use at most 64 MiB of HBM per device.

v0:
```python
import jax
import jax.numpy as jnp
from jax import lax
from jax.sharding import PartitionSpec as P

H = 8
STEPS = 2


def passed_along(block, axis, distance):
    devices = range(lax.axis_size(axis))
    route = [((i - distance) % len(devices), i) for i in devices]
    return lax.ppermute(block, axis, route)


def broadcast(shard, axis, root):
    mine = lax.axis_index(axis) == root
    return lax.psum(jnp.where(mine, shard, jnp.zeros_like(shard)), axis)


def band_ranks(values):
    live = values >= 0
    same = values[None, :] == values[:, None]
    earlier = jnp.tril(same, -1)
    first = live & jnp.logical_not(jnp.any(earlier, axis=1))
    below = first[None, :] & (values[None, :] < values[:, None])
    return jnp.sum(below.astype(jnp.int32), axis=1)


def grid_cells(coords):
    row_rank = band_ranks(coords[0])
    col_rank = band_ranks(coords[1])
    live = coords[0] >= 0
    return jnp.where(live, row_rank * H + col_rank, H * H)


def dense_tile(blocks, coords):
    slot_count = coords.shape[1]
    cells = grid_cells(coords)
    hits = cells[None, :] == jnp.arange(H * H, dtype=jnp.int32)[:, None]
    present = jnp.any(hits, axis=1)
    slot_of = jnp.sum(
        hits.astype(jnp.int32) * jnp.arange(slot_count, dtype=jnp.int32)[None, :], axis=1
    )
    picked = jnp.where(present[:, None, None], blocks[slot_of], jnp.zeros((), blocks.dtype))
    width = blocks.shape[1]
    return picked.reshape(H, H, width, width).transpose(0, 2, 1, 3).reshape(H * width, H * width)


def tile_product(a_blocks, a_coords, b_blocks, b_coords, o_coords):
    width = a_blocks.shape[1]
    left_grid = dense_tile(a_blocks, a_coords)
    right_grid = dense_tile(b_blocks, b_coords)
    whole = jnp.dot(left_grid, right_grid, preferred_element_type=jnp.float32)
    cell_blocks = (
        whole.reshape(H, width, H, width).transpose(0, 2, 1, 3).reshape(H * H, width, width)
    )
    cells = grid_cells(o_coords)
    live = cells < H * H
    taken = cell_blocks[jnp.minimum(cells, H * H - 1)]
    return jnp.where(live[:, None, None], taken, jnp.zeros((), jnp.float32))


def body(x_blocks, x_coords):
    blocks = x_blocks[0, 0]
    coords = x_coords[0, 0]
    band_count = lax.axis_size("col")
    band_i = lax.axis_index("col")
    layer_at = lax.axis_index("layer")
    layer_count = lax.axis_size("layer")
    right_blocks = blocks
    right_coords = coords
    moved_blocks, moved_coords = passed_along((blocks, coords), "col", -1 * STEPS)
    chosen = layer_at == 1
    right_blocks = jnp.where(chosen, moved_blocks, right_blocks)
    right_coords = jnp.where(chosen, moved_coords, right_coords)
    summed = jnp.zeros(blocks.shape, jnp.float32)
    for step_at in range(STEPS):
        root_at = (band_i + layer_at * STEPS + step_at) % band_count
        left_blocks, left_coords = (
            broadcast(blocks, "row", root_at),
            broadcast(coords, "row", root_at),
        )
        summed = summed + tile_product(left_blocks, left_coords, right_blocks, right_coords, coords)
        if step_at + 1 < STEPS:
            right_blocks, right_coords = passed_along((right_blocks, right_coords), "col", -1)
    share_rows = summed.shape[0] // layer_count
    layer_sum = lax.psum(summed, "layer")
    kept_part = lax.dynamic_slice_in_dim(layer_sum, layer_at * share_rows, share_rows, 0)
    return kept_part[None, None]


def solution(mesh):
    return jax.shard_map(
        body,
        mesh=mesh,
        in_specs=(P("col", "row", None, None, None), P("col", "row", None, None)),
        out_specs=P("col", "row", "layer", None, None),
        check_vma=False,
    )
```

profile of v0, /device:TPU:1, one launch (start us, length us, event | category | flops | bytes accessed | tf_op | source)
XLA Modules:
  0.0 367.6 jit_solution(3304556697250064698)
XLA Ops:
  6.5 12.4 %collective-permute-start = (s32[2,32]{1,0:T(2,128)}, s32[2,32]{1,0:T(2,128)S(1)}, u32[]{:S(2)}, u32[]{:S(2)}) collective-permute-start(s32[2,32]{1,0:T(2,128)} %bitcast.191), channel_id=1, source_target_pairs={{2,0},{3,1},{4,2},{5,3},{6,4},{7,5},{8,6},{9,7},{10,8},{11,9},{12,... | collective-permute-start | bytes 776 | tf_op jit(solution)/shard_map/ppermute | solution.py:13
  18.9 3.1 collective-permute-start.1
  22.0 0.8 slice_bitcast_fusion.5
  22.8 0.7 broadcast_select_fusion.3
  23.5 3.8 %collective-permute-start.2 = (s32[2,32]{1,0:T(2,128)S(1)}, s32[2,32]{1,0:T(2,128)S(1)}, u32[]{:S(2)}, u32[]{:S(2)}) collective-permute-start(s32[2,32]{1,0:T(2,128)S(1)} %get-tuple-element.44), channel_id=1, source_target_pairs={{1,0},{2,1},{3,2},{4,3},{5,4},{6,5},{7,6},{8,7},{9,8},{10,9},{11,1... | collective-permute-start | bytes 776 | tf_op jit(solution)/shard_map/ppermute | solution.py:13
  27.4 12.8 %all-reduce = (s32[2,32]{1,0:T(2,128)S(1)}, s32[2,32]{1,0:T(2,128)S(1)}) all-reduce(s32[2,32]{1,0:T(2,128)S(1)} %get-tuple-element.43, s32[2,32]{1,0:T(2,128)S(1)} %get-tuple-element.42), channel_id=1, replica_groups=mesh['layer'=2,'row'=16,'col'=16] {'row'}, use_global_device_ids=true, to_apply=%region_4.5 | all-reduce | flops 128 | bytes 1024 | tf_op jit(solution)/shard_map/psum | solution.py:18
  40.2 26.5 %collective-permute-done.2 = s32[2,32]{1,0:T(2,128)S(1)} collective-permute-done((s32[2,32]{1,0:T(2,128)S(1)}, s32[2,32]{1,0:T(2,128)S(1)}, u32[]{:S(2)}, u32[]{:S(2)}) %collective-permute-start.2) | collective-permute-done | bytes 288 | tf_op jit(solution)/shard_map/ppermute | solution.py:13
  68.7 0.8 not_and_fusion.1
  69.8 0.7 fusion.46
  70.5 2.8 broadcast_select_fusion.2
  73.5 5.1 %collective-permute-start.3 = (bf16[32,128,128]{2,1,0:T(8,128)(2,1)S(1)}, bf16[32,128,128]{2,1,0:T(8,128)(2,1)}, u32[]{:S(2)}, u32[]{:S(2)}) collective-permute-start(bf16[32,128,128]{2,1,0:T(8,128)(2,1)S(1)} %get-tuple-element.20), channel_id=1, source_target_pairs={{1,0},{2,1},{3,2},{4,3},{5,4},{6,5},{7,6},{8,7},{9,8},{10,9},{11,1... | collective-permute-start | bytes 3145736 | tf_op jit(solution)/shard_map/ppermute | solution.py:13
  79.0 1.0 gather_fusion.1
  80.0 1.3 copy_select_fusion.2
  82.0 2.8 copy.19
  84.8 15.2 %collective-permute-done.3 = bf16[32,128,128]{2,1,0:T(8,128)(2,1)} collective-permute-done((bf16[32,128,128]{2,1,0:T(8,128)(2,1)S(1)}, bf16[32,128,128]{2,1,0:T(8,128)(2,1)}, u32[]{:S(2)}, u32[]{:S(2)}) %collective-permute-start.3) | collective-permute-done | bytes 1048608 | tf_op jit(solution)/shard_map/ppermute | solution.py:13
  99.9 2.2 gather_fusion.4
  102.1 1.3 copy_select_fusion
  104.1 2.6 copy.20
  106.7 125.7 %all-reduce.7.cloned.1.call-done = (bf16[32,128,128]{2,1,0:T(8,128)(2,1)}, bf16[32,128,128]{2,1,0:T(8,128)(2,1)}) async-done(((bf16[32,128,128]{2,1,0:T(8,128)(2,1)}, bf16[32,128,128]{2,1,0:T(8,128)(2,1)}), (bf16[32,128,128]{2,1,0:T(8,128)(2,1)}, bf16[32,128,128]{2,1,0:T(8,128)(2,1)})) %all-reduce.7.cloned.1.call-update) | async-done | bytes 2097168 | tf_op jit(solution)/shard_map/psum | solution.py:18
  232.4 2.2 gather_fusion
  234.6 2.6 fusion.5
  237.2 4.3 %reshape.371 = bf16[8,128,1024,1]{2,1,0,3:T(8,128)(2,1)} reshape(bf16[8,128,8,128]{3,2,1,0:T(8,128)(2,1)} %fusion.5) | data formatting | bytes 4194304 | tf_op jit(solution)/shard_map/dot_general | solution.py:54
  241.5 0.9 gather_fusion.3
  242.5 2.6 fusion.4
  245.1 4.3 %reshape.373 = bf16[8,128,1024,1]{2,1,0,3:T(8,128)(2,1)} reshape(bf16[8,128,8,128]{3,2,1,0:T(8,128)(2,1)} %fusion.4) | data formatting | bytes 4194304 | tf_op jit(solution)/shard_map/dot_general | solution.py:54
  249.4 5.5 %fusion.2 = f32[8,128,8,128]{3,1,2,0:T(8,128)} fusion(bf16[8,128,1024,1]{2,1,0,3:T(8,128)(2,1)S(1)} %bitcast.186, bf16[8,128,1024,1]{2,1,0,3:T(8,128)(2,1)} %reshape.371), kind=kOutput, calls=%fused_computation.10 | convolution fusion | flops 2147483648 | bytes 8388608 | tf_op jit(solution)/shard_map/dot_general | solution.py:54
  255.0 2.9 gather_fusion.2
  257.8 6.5 %fusion = f32[8,128,8,128]{3,1,2,0:T(8,128)} fusion(bf16[8,128,1024,1]{2,1,0,3:T(8,128)(2,1)} %bitcast.187, bf16[8,128,1024,1]{2,1,0,3:T(8,128)(2,1)} %reshape.373), kind=kOutput, calls=%fused_computation.8 | convolution fusion | flops 2147483648 | bytes 8388608 | tf_op jit(solution)/shard_map/dot_general | solution.py:54
  264.4 4.2 %gather_fusion.5 = f32[32,128,128]{2,1,0:T(8,128)} fusion(f32[64,128,128]{2,1,0:T(8,128)} %bitcast.188, s32[1024]{0:T(1024)S(1)} %pad_clamp_fusion.2), kind=kCustom, calls=%fused_computation.5 | custom fusion | bytes 4194432 | tf_op jit(solution)/shard_map/gather | solution.py:60
  268.6 3.4 select_add_fusion
  272.0 86.4 %all-reduce.5.cloned.1.call-done = f32[32,128,128]{2,1,0:T(8,128)} async-done(((f32[32,128,128]{2,1,0:T(8,128)}), f32[32,128,128]{2,1,0:T(8,128)}) %all-reduce.5.cloned.1.call-update) | async-done | bytes 2097168 | tf_op jit(solution)/shard_map/psum | solution.py:88
  358.4 2.3 dynamic-slice_bitcast_fusion
  (56 shorter events, 4.2 us)
Async XLA Ops:
  6.5 225.9 %all-reduce.7.cloned.1.call-start = ((), (), s32[]{:S(2)}) async-start(), calls=%async_computation.1 | async-start | bytes 4194304 | tf_op jit(solution)/shard_map/psum | solution.py:18
  6.5 16.3 %collective-permute-start = (s32[2,32]{1,0:T(2,128)}, s32[2,32]{1,0:T(2,128)S(1)}, u32[]{:S(2)}, u32[]{:S(2)}) collective-permute-start(s32[2,32]{1,0:T(2,128)} %bitcast.191), channel_id=1, source_target_pairs={{2,0},{3,1},{4,2},{5,3},{6,4},{7,5},{8,6},{9,7},{10,8},{11,9},{12,... | collective-permute-start | bytes 776 | tf_op jit(solution)/shard_map/ppermute | solution.py:13
  18.9 51.6 %collective-permute-start.1 = (bf16[32,128,128]{2,1,0:T(8,128)(2,1)}, bf16[32,128,128]{2,1,0:T(8,128)(2,1)S(1)}, u32[]{:S(2)}, u32[]{:S(2)}) collective-permute-start(bf16[32,128,128]{2,1,0:T(8,128)(2,1)} %bitcast.190), channel_id=1, source_target_pairs={{2,0},{3,1},{4,2},{5,3},{6,4},{7,5},{8,6},{9,7},{10,8},{11,9},{12,... | collective-permute-start | bytes 3145736 | tf_op jit(solution)/shard_map/ppermute | solution.py:13
  23.5 43.2 %collective-permute-start.2 = (s32[2,32]{1,0:T(2,128)S(1)}, s32[2,32]{1,0:T(2,128)S(1)}, u32[]{:S(2)}, u32[]{:S(2)}) collective-permute-start(s32[2,32]{1,0:T(2,128)S(1)} %get-tuple-element.44), channel_id=1, source_target_pairs={{1,0},{2,1},{3,2},{4,3},{5,4},{6,5},{7,6},{8,7},{9,8},{10,9},{11,1... | collective-permute-start | bytes 776 | tf_op jit(solution)/shard_map/ppermute | solution.py:13
  73.3 5.8 %copy-start.2 = (s32[1,1,2,32]{3,2,1,0:T(2,128)S(1)}, s32[1,1,2,32]{3,2,1,0:T(2,128)}, u32[]{:S(2)}) copy-start(s32[1,1,2,32]{3,2,1,0:T(2,128)} %param.3) | copy-start | bytes 772
  73.3 285.1 %all-reduce.5.cloned.1.call-start = ((), (), s32[]{:S(2)}) async-start(), calls=%async_computation | async-start | bytes 4194304 | tf_op jit(solution)/shard_map/psum | solution.py:88
  73.5 26.5 %collective-permute-start.3 = (bf16[32,128,128]{2,1,0:T(8,128)(2,1)S(1)}, bf16[32,128,128]{2,1,0:T(8,128)(2,1)}, u32[]{:S(2)}, u32[]{:S(2)}) collective-permute-start(bf16[32,128,128]{2,1,0:T(8,128)(2,1)S(1)} %get-tuple-element.20), channel_id=1, source_target_pairs={{1,0},{2,1},{3,2},{4,3},{5,4},{6,5},{7,6},{8,7},{9,8},{10,9},{11,1... | collective-permute-start | bytes 3145736 | tf_op jit(solution)/shard_map/ppermute | solution.py:13
  237.2 4.3 %copy-start = (bf16[32,128,128]{2,1,0:T(8,128)(2,1)S(1)}, bf16[32,128,128]{2,1,0:T(8,128)(2,1)}, u32[]{:S(2)}) copy-start(bf16[32,128,128]{2,1,0:T(8,128)(2,1)} %get-tuple-element.17) | copy-start | bytes 3145732
  245.1 4.3 %copy-start.1 = (bf16[1024,1024]{1,0:T(8,128)(2,1)S(1)}, bf16[1024,1024]{1,0:T(8,128)(2,1)}, u32[]{:S(2)}) copy-start(bf16[1024,1024]{1,0:T(8,128)(2,1)} %copy.19) | copy-start | bytes 6291460
Sparse Core Ops, SparseCore 0:
  73.4 158.9 all-reduce.6
  272.1 86.2 all-reduce.4
where the time goes:
time: 368 us
  waiting for transfers between devices  254 us (69%)
  local copies, waits for them, and re-layouts  31.9 us (9%)
  starting transfers between devices  24.4 us (7%)
  other arithmetic  18.7 us (5%)
  between operations  13.7 us (4%)
  blocking collectives  12.8 us (3%)
  matrix products  12 us (3%)
    psum x1, waiting for transfers between devices, broadcast(): return lax.psum(jnp.where(mine, shard, jnp.zeros_like(shard)), axis)  126 us
    psum x1, waiting for transfers between devices, body(): layer_sum = lax.psum(summed, 'layer')  86.4 us
    ppermute x4, waiting for transfers between devices, passed_along(): return lax.ppermute(block, axis, route)  41.7 us
    ppermute x4, starting transfers between devices, passed_along(): return lax.ppermute(block, axis, route)  24.4 us
    dot_general x4, local copies, waits for them, and re-layouts, tile_product(): whole = jnp.dot(left_grid, right_grid, preferred_element_type=jnp.float32)  14 us
    psum x1, blocking collectives, broadcast(): return lax.psum(jnp.where(mine, shard, jnp.zeros_like(shard)), axis)  12.8 us
    dot_general x2, matrix products, tile_product(): whole = jnp.dot(left_grid, right_grid, preferred_element_type=jnp.float32)  12 us
  transfers between devices with their start and end apart: 6, of which 4 were waited for; matrix products, arithmetic and copies ran while one was open for 5% of the time, Pallas kernels for 0%

commit v1 on v0

v1 whole, which is shorter than its diff:
```python
import functools

import jax
import jax.numpy as jnp
from jax import lax
from jax.experimental import pallas as pl
from jax.experimental.pallas import tpu as pltpu
from jax.sharding import PartitionSpec as P

H = 8
STEPS = 4
W = 128
GROUP = 8
ROWS = GROUP * W
PACK = ROWS + 16
DENSE = H * W
AXES = ("layer", "row", "col")


def pairs_of(mesh_shape, target):
    layers, rows, cols = mesh_shape
    flat = lambda at: (at[0] * rows + at[1]) * cols + at[2]
    found = []
    for l in range(layers):
        for r in range(rows):
            for c in range(cols):
                to = target(l, r, c)
                if to is not None:
                    found.append((flat((l, r, c)), flat(to)))
    return found


def cells_and_table(coords):
    slots = coords.shape[1]
    values = jnp.arange(W, dtype=jnp.int32)
    used = jnp.any(coords[:, :, None] == values[None, None, :], axis=1)
    below = used[:, None, :] & (values[None, None, :] < coords[:, :, None])
    rank = jnp.sum(below.astype(jnp.int32), axis=2)
    cells = jnp.where(coords[0] >= 0, rank[0] * H + rank[1], H * H)
    hits = cells[None, :] == values[:, None]
    order = jnp.arange(slots, dtype=jnp.int32) - slots
    table = slots + jnp.sum(jnp.where(hits, order[None, :], 0), axis=1)
    return cells, table


def kernel(own_table, own_cells, meta, own, *refs):
    n_left = 10
    left = refs[:n_left]
    right = refs[n_left:n_left + 12]
    out = refs[n_left + 12]
    (a_all, b_all, a_head, b_head, table_v, table_s, a_dense, b_dense, prod, sems) = refs[n_left + 13:]
    copies = []

    def start(src, dst):
        c = pltpu.make_async_copy(src, dst, sems.at[len(copies)])
        c.start()
        copies.append(c)

    at = 0
    for ref in left:
        for e in range(ref.shape[0]):
            place = meta[at]
            step, part = place // 4, place % 4
            start(ref.at[e, pl.ds(0, ROWS)], a_all.at[step, pl.ds(part * ROWS, ROWS)])
            start(ref.at[e, pl.ds(ROWS, 16)], a_head.at[place])
            at += 1
    start(own, b_all.at[0, pl.ds(0, 4 * ROWS)])
    for s in range(1, STEPS):
        for g in range(4):
            place = meta[16 + g]
            ref = right[(s - 1) * 4 + g]
            start(ref.at[pl.ds(0, ROWS)], b_all.at[s, pl.ds(place * ROWS, ROWS)])
            start(ref.at[pl.ds(ROWS, 16)], b_head.at[(s - 1) * 4 + place])
    zero = jnp.zeros((W, W), jnp.bfloat16)
    for s in range(STEPS):
        a_all[s, 4 * ROWS:, :] = zero
        b_all[s, 4 * ROWS:, :] = zero
    for c in copies:
        c.wait()
    for s in range(STEPS):
        table_v[s:s + 1, :] = a_head[4 * s, 0:1, :].astype(jnp.float32).astype(jnp.int32)
        if s:
            table_v[4 + s:5 + s, :] = b_head[4 * (s - 1), 0:1, :].astype(jnp.float32).astype(jnp.int32)
        else:
            table_v[4:5, :] = jnp.zeros((1, W), jnp.int32)
    last = pltpu.make_async_copy(table_v, table_s, sems.at[len(copies)])
    last.start()
    last.wait()

    @pl.loop(0, W)
    def _(i):
        table_s[4, i] = own_table[i]

    @pl.loop(0, STEPS)
    def _(s):
        for r in range(H):
            for k in range(H):
                slot = table_s[s, r * H + k]
                rows = pl.ds(pl.multiple_of(slot * W, W), W)
                a_dense[s, r * W:(r + 1) * W, k * W:(k + 1) * W] = a_all[s, rows, :]
                slot = table_s[4 + s, r * H + k]
                rows = pl.ds(pl.multiple_of(slot * W, W), W)
                b_dense[s, k // 2, r * W:(r + 1) * W, (k % 2) * W:(k % 2 + 1) * W] = b_all[s, rows, :]

    @pl.loop(0, 4)
    def _(n):
        total = jnp.dot(a_dense[0], b_dense[0, n], preferred_element_type=jnp.float32)
        for s in range(1, STEPS):
            total += jnp.dot(a_dense[s], b_dense[s, n], preferred_element_type=jnp.float32)
        prod[2 * n] = total[:, :W]
        prod[2 * n + 1] = total[:, W:]

    base = meta[20]

    @pl.loop(0, 16)
    def _(q):
        cell = own_cells[base + q]
        live = cell < H * H
        held = jnp.where(live, cell, 0)
        rows = pl.ds(pl.multiple_of((held // H) * W, W), W)
        block = prod[held % H, rows, :]
        out[q] = jnp.where(live, block, jnp.zeros_like(block))


def body(mesh_shape, x_blocks, x_coords):
    blocks = x_blocks[0, 0].reshape(4, ROWS, W)
    coords = x_coords[0, 0]
    _, rows, cols = mesh_shape
    layer, row, col = (lax.axis_index(a) for a in AXES)
    cells, table = cells_and_table(coords)
    head = jnp.broadcast_to(table.astype(jnp.bfloat16)[None, None, :], (4, 16, W))
    packed = jnp.concatenate([blocks, head], axis=1)

    def send(value, target):
        return lax.ppermute(value, AXES, pairs_of(mesh_shape, target))

    down = lambda l, r, c: (l, r, (c - 1) % cols)
    over = lambda l, r, c: (1 - l, r, c)
    mine = lax.dynamic_slice_in_dim(packed, 2 * layer, 2, 0)
    chunk = [mine[0], mine[1]]
    right = []
    for s in range(1, STEPS):
        chunk = [send(v, down) for v in chunk]
        right += chunk + [send(v, over) for v in chunk]

    place = (row - col) % rows
    part_at = place // 4
    piece = packed[0]
    for t in range(1, 4):
        got = send(packed[t], lambda l, r, c: (l, (r + 4 * t) % rows, c) if (r - c) % rows < 4 else None)
        piece = jnp.where(part_at == t, got, piece)
    cross = send(piece, lambda l, r, c: (1 - l, r ^ 2, c))
    here = jnp.stack([piece, cross])
    y_up = lambda l, r, c: (l, (r + 4) % rows, c)
    y_dn = lambda l, r, c: (l, (r - 4) % rows, c)
    from_dn = send(here, y_up)
    from_up = send(here, y_dn)
    far0 = send(from_up[0], y_dn)
    far1 = send(from_dn[1], y_up)
    left = [here, from_dn, from_up, far0[None], far1[None]]
    twin = lambda l, r, c: (l, r ^ 1, c)
    left += [send(v, twin) for v in left]
    places = []
    for me in (row, row ^ 1):
        for r, es in ((me, (0, 1)), ((me - 4) % rows, (0, 1)), ((me + 4) % rows, (0, 1)), ((me + 8) % rows, (0, 1))):
            for e in es:
                d = ((r ^ 2 if e else r) - col) % rows
                places.append((d % 4) * 4 + d // 4)
    own_half, other_half = 2 * layer, 2 * (1 - layer)
    meta = jnp.stack(places + [own_half, own_half + 1, other_half, other_half + 1, 16 * layer]).astype(jnp.int32)

    any_space = pl.BlockSpec(memory_space=pl.ANY)
    smem = pl.BlockSpec(memory_space=pltpu.SMEM)
    ops = left + right
    result = pl.pallas_call(
        kernel,
        out_shape=jax.ShapeDtypeStruct((16, W, W), jnp.float32),
        in_specs=[smem] * 3 + [any_space] * (1 + len(ops)),
        out_specs=pl.BlockSpec(memory_space=pltpu.VMEM),
        scratch_shapes=[
            pltpu.VMEM((STEPS, 33 * W, W), jnp.bfloat16),
            pltpu.VMEM((STEPS, 33 * W, W), jnp.bfloat16),
            pltpu.VMEM((16, 16, W), jnp.bfloat16),
            pltpu.VMEM((12, 16, W), jnp.bfloat16),
            pltpu.VMEM((8, W), jnp.int32),
            pltpu.SMEM((8, W), jnp.int32),
            pltpu.VMEM((STEPS, DENSE, DENSE), jnp.bfloat16),
            pltpu.VMEM((STEPS, 4, DENSE, 2 * W), jnp.bfloat16),
            pltpu.VMEM((H, DENSE, W), jnp.float32),
            pltpu.SemaphoreType.DMA((64,)),
        ],
        compiler_params=pltpu.CompilerParams(vmem_limit_bytes=48 * 1024 * 1024),
    )(table, cells, meta, x_blocks.reshape(4 * ROWS, W), *ops)
    return result[None, None]


def solution(mesh):
    return jax.shard_map(
        functools.partial(body, tuple(mesh.shape[a] for a in AXES)),
        mesh=mesh,
        in_specs=(P("col", "row", None, None, None), P("col", "row", None, None)),
        out_specs=P("col", "row", "layer", None, None),
        check_vma=False,
    )
```

time: 368 us -> 129 us (0.35)
  waiting for transfers between devices: 254 us -> 5.54 us
  starting transfers between devices: 24.4 us -> 89.7 us
  local copies, waits for them, and re-layouts: 31.9 us -> 7.7 us
  Pallas kernels: 0 us -> 19.4 us
  other arithmetic: 18.7 us -> 3.92 us
  blocking collectives: 12.8 us -> 0 us
  between operations: 13.7 us -> 1.6 us
  matrix products: 12 us -> 0 us
    psum x2 -> x0, waiting for transfers between devices: 212 us -> none  [the longest x1 126 us: broadcast(): return lax.psum(jnp.where(mine, shard, jnp.zeros_like(shard)), axis)]
    ppermute x4 -> x25, starting transfers between devices: 24.4 us -> 89.7 us  [send(): return lax.ppermute(value, AXES, pairs_of(mesh_shape, target))]
    ppermute x4 -> x25, waiting for transfers between devices: 41.7 us -> 5.54 us  [send(): return lax.ppermute(value, AXES, pairs_of(mesh_shape, target))]
    pallas_call x0 -> x1, Pallas kernels: none -> 19.4 us  [body(): pl.pallas_call(kernel, out_shape=jax.ShapeDtypeStruct((16, W, W), jnp.flo...]
    dot_general x4 -> x0, local copies, waits for them, and re-layouts: 14 us -> none  [tile_product(): whole = jnp.dot(left_grid, right_grid, preferred_element_type=jnp.float32)]
    gather x6 -> x0, local copies, waits for them, and re-layouts: 13.3 us -> none  [the longest x2 7.06 us: tile_product(): taken = cell_blocks[jnp.minimum(cells, H * H - 1)]]
    psum x1 -> x0, blocking collectives: 12.8 us -> none  [broadcast(): return lax.psum(jnp.where(mine, shard, jnp.zeros_like(shard)), axis)]
    dot_general x2 -> x0, matrix products: 12 us -> none  [tile_product(): whole = jnp.dot(left_grid, right_grid, preferred_element_type=jnp.float32)]
  transfers between devices with their start and end apart: 6 -> 25, of which waited for: 4 -> 3; matrix products, arithmetic and copies ran while one was open for 5% -> 0% of each run, Pallas kernels for 0% -> 0%
where the time goes in v1:
time: 129 us; the launch traced here: 128 us
  starting transfers between devices  89.7 us (70%)
  Pallas kernels  19.4 us (15%)
  local copies, waits for them, and re-layouts  7.7 us (6%)
  waiting for transfers between devices  5.54 us (4%)
  other arithmetic  3.92 us (3%)
  between operations  1.6 us (1%)
    ppermute x25, starting transfers between devices, send(): return lax.ppermute(value, AXES, pairs_of(mesh_shape, target))  89.7 us
    pallas_call x1, Pallas kernels, body(): pl.pallas_call(kernel, out_shape=jax.ShapeDtypeStruct((16, W, W), jnp.flo...  19.4 us
    unnamed x24, local copies, waits for them, and re-layouts  7.52 us
    ppermute x25, waiting for transfers between devices, send(): return lax.ppermute(value, AXES, pairs_of(mesh_shape, target))  5.54 us
  transfers between devices with their start and end apart: 25, of which 3 were waited for; matrix products, arithmetic and copies ran while one was open for 0% of the time, Pallas kernels for 0%

profile of v1, /device:TPU:1, one launch (start us, length us, event | category | flops | bytes accessed | tf_op | source)
XLA Modules:
  0.0 127.8 jit_solution(4906920783015449198)
XLA Ops:
  2.5 1.2 fusion.9
  3.7 4.0 %collective-permute-start.2 = (bf16[1040,128]{1,0:T(8,128)(2,1)S(1)}, bf16[1040,128]{1,0:T(8,128)(2,1)S(1)}, u32[]{:S(2)}, u32[]{:S(2)}) collective-permute-start(bf16[1040,128]{1,0:T(8,128)(2,1)S(1)} %get-tuple-element.5), channel_id=1, source_target_pairs={{0,64},{13,77},{14,78},{15,79},{16,80},{17,81},{30,94},{31,95},{32... | collective-permute-start | bytes 798728 | tf_op jit(solution)/shard_map/ppermute | solution.py:135
  7.7 2.1 %collective-permute-start = (bf16[1040,128]{1,0:T(8,128)(2,1)S(1)}, bf16[1040,128]{1,0:T(8,128)(2,1)S(1)}, u32[]{:S(2)}, u32[]{:S(2)}) collective-permute-start(bf16[1040,128]{1,0:T(8,128)(2,1)S(1)} %get-tuple-element.6), channel_id=1, source_target_pairs={{0,192},{13,205},{14,206},{15,207},{16,208},{17,209},{30,222},{31,... | collective-permute-start | bytes 798728 | tf_op jit(solution)/shard_map/ppermute | solution.py:135
  9.9 1.3 %collective-permute-start.1 = (bf16[1040,128]{1,0:T(8,128)(2,1)S(1)}, bf16[1040,128]{1,0:T(8,128)(2,1)S(1)}, u32[]{:S(2)}, u32[]{:S(2)}) collective-permute-start(bf16[1040,128]{1,0:T(8,128)(2,1)S(1)} %get-tuple-element.7), channel_id=1, source_target_pairs={{0,128},{13,141},{14,142},{15,143},{16,144},{17,145},{30,158},{31,... | collective-permute-start | bytes 798728 | tf_op jit(solution)/shard_map/ppermute | solution.py:135
  11.3 1.9 %collective-permute-done = bf16[1040,128]{1,0:T(8,128)(2,1)S(1)} collective-permute-done((bf16[1040,128]{1,0:T(8,128)(2,1)S(1)}, bf16[1040,128]{1,0:T(8,128)(2,1)S(1)}, u32[]{:S(2)}, u32[]{:S(2)}) %collective-permute-start) | collective-permute-done | bytes 266272 | tf_op jit(solution)/shard_map/ppermute | solution.py:135
  13.2 3.3 %collective-permute-done.1 = bf16[1040,128]{1,0:T(8,128)(2,1)S(1)} collective-permute-done((bf16[1040,128]{1,0:T(8,128)(2,1)S(1)}, bf16[1040,128]{1,0:T(8,128)(2,1)S(1)}, u32[]{:S(2)}, u32[]{:S(2)}) %collective-permute-start.1) | collective-permute-done | bytes 266272 | tf_op jit(solution)/shard_map/ppermute | solution.py:135
  16.6 6.4 %collective-permute-start.3 = (bf16[1040,128]{1,0:T(8,128)(2,1)S(1)}, bf16[1040,128]{1,0:T(8,128)(2,1)S(1)}, u32[]{:S(2)}, u32[]{:S(2)}) collective-permute-start(bf16[1040,128]{1,0:T(8,128)(2,1)S(1)} %fusion.8), channel_id=1, source_target_pairs={{0,288},{1,289},{2,290},{3,291},{4,292},{5,293},{6,294},{7,295},{8... | collective-permute-start | bytes 798728 | tf_op jit(solution)/shard_map/ppermute | solution.py:135
  23.1 8.7 %collective-permute-start.14 = (bf16[1040,128]{1,0:T(8,128)(2,1)S(1)}, bf16[1040,128]{1,0:T(8,128)(2,1)S(1)}, u32[]{:S(2)}, u32[]{:S(2)}) collective-permute-start(bf16[1040,128]{1,0:T(8,128)(2,1)S(1)} %get-tuple-element.8), channel_id=1, source_target_pairs={{0,15},{1,0},{2,1},{3,2},{4,3},{5,4},{6,5},{7,6},{8,7},{9,8},{10,9... | collective-permute-start | bytes 798728 | tf_op jit(solution)/shard_map/ppermute | solution.py:135
  31.7 2.6 %collective-permute-start.13 = (bf16[1040,128]{1,0:T(8,128)(2,1)S(1)}, bf16[1040,128]{1,0:T(8,128)(2,1)S(1)}, u32[]{:S(2)}, u32[]{:S(2)}) collective-permute-start(bf16[1040,128]{1,0:T(8,128)(2,1)S(1)} %get-tuple-element.9), channel_id=1, source_target_pairs={{0,15},{1,0},{2,1},{3,2},{4,3},{5,4},{6,5},{7,6},{8,7},{9,8},{10,9... | collective-permute-start | bytes 798728 | tf_op jit(solution)/shard_map/ppermute | solution.py:135
  34.5 7.1 %collective-permute-start.5 = (bf16[2,1040,128]{2,1,0:T(8,128)(2,1)S(1)}, bf16[2,1040,128]{2,1,0:T(8,128)(2,1)S(1)}, u32[]{:S(2)}, u32[]{:S(2)}) collective-permute-start(bf16[2,1040,128]{2,1,0:T(8,128)(2,1)S(1)} %pad_maximum_fusion.refs_0_), channel_id=1, source_target_pairs={{0,192},{1,193},{2,194},{3,195},{4,196},{5,197},{6,198},{7,199},{8... | collective-permute-start | bytes 1597448 | tf_op jit(solution)/shard_map/ppermute | solution.py:135
  41.5 2.6 %collective-permute-start.18 = (bf16[1040,128]{1,0:T(8,128)(2,1)S(1)}, bf16[1040,128]{1,0:T(8,128)(2,1)S(1)}, u32[]{:S(2)}, u32[]{:S(2)}) collective-permute-start(bf16[1040,128]{1,0:T(8,128)(2,1)S(1)} %collective-permute-done.14.refs_11_), channel_id=1, source_target_pairs={{0,15},{1,0},{2,1},{3,2},{4,3},{5,4},{6,5},{7,6},{8,7},{9,8},{10,9... | collective-permute-start | bytes 798728 | tf_op jit(solution)/shard_map/ppermute | solution.py:135
  44.2 2.7 %collective-permute-start.17 = (bf16[1040,128]{1,0:T(8,128)(2,1)S(1)}, bf16[1040,128]{1,0:T(8,128)(2,1)S(1)}, u32[]{:S(2)}, u32[]{:S(2)}) collective-permute-start(bf16[1040,128]{1,0:T(8,128)(2,1)S(1)} %collective-permute-done.13.refs_10_), channel_id=1, source_target_pairs={{0,15},{1,0},{2,1},{3,2},{4,3},{5,4},{6,5},{7,6},{8,7},{9,8},{10,9... | collective-permute-start | bytes 798728 | tf_op jit(solution)/shard_map/ppermute | solution.py:135
  46.9 5.4 %collective-permute-start.4 = (bf16[2,1040,128]{2,1,0:T(8,128)(2,1)S(1)}, bf16[2,1040,128]{2,1,0:T(8,128)(2,1)S(1)}, u32[]{:S(2)}, u32[]{:S(2)}) collective-permute-start(bf16[2,1040,128]{2,1,0:T(8,128)(2,1)S(1)} %pad_maximum_fusion.refs_0_), channel_id=1, source_target_pairs={{0,64},{1,65},{2,66},{3,67},{4,68},{5,69},{6,70},{7,71},{8,72},{9,... | collective-permute-start | bytes 1597448 | tf_op jit(solution)/shard_map/ppermute | solution.py:135
  52.3 1.9 %collective-permute-start.16 = (bf16[1040,128]{1,0:T(8,128)(2,1)S(1)}, bf16[1040,128]{1,0:T(8,128)(2,1)S(1)}, u32[]{:S(2)}, u32[]{:S(2)}) collective-permute-start(bf16[1040,128]{1,0:T(8,128)(2,1)S(1)} %collective-permute-done.14.refs_11_), channel_id=1, source_target_pairs={{0,256},{1,257},{2,258},{3,259},{4,260},{5,261},{6,262},{7,263},{8... | collective-permute-start | bytes 798728 | tf_op jit(solution)/shard_map/ppermute | solution.py:135
  54.2 3.4 %collective-permute-start.15 = (bf16[1040,128]{1,0:T(8,128)(2,1)S(1)}, bf16[1040,128]{1,0:T(8,128)(2,1)S(1)}, u32[]{:S(2)}, u32[]{:S(2)}) collective-permute-start(bf16[1040,128]{1,0:T(8,128)(2,1)S(1)} %collective-permute-done.13.refs_10_), channel_id=1, source_target_pairs={{0,256},{1,257},{2,258},{3,259},{4,260},{5,261},{6,262},{7,263},{8... | collective-permute-start | bytes 798728 | tf_op jit(solution)/shard_map/ppermute | solution.py:135
  57.6 4.1 %collective-permute-start.22 = (bf16[1040,128]{1,0:T(8,128)(2,1)S(1)}, bf16[1040,128]{1,0:T(8,128)(2,1)S(1)}, u32[]{:S(2)}, u32[]{:S(2)}) collective-permute-start(bf16[1040,128]{1,0:T(8,128)(2,1)S(1)} %collective-permute-done.18.refs_15_), channel_id=1, source_target_pairs={{0,15},{1,0},{2,1},{3,2},{4,3},{5,4},{6,5},{7,6},{8,7},{9,8},{10,9... | collective-permute-start | bytes 798728 | tf_op jit(solution)/shard_map/ppermute | solution.py:135
  61.7 2.6 %collective-permute-start.21 = (bf16[1040,128]{1,0:T(8,128)(2,1)S(1)}, bf16[1040,128]{1,0:T(8,128)(2,1)S(1)}, u32[]{:S(2)}, u32[]{:S(2)}) collective-permute-start(bf16[1040,128]{1,0:T(8,128)(2,1)S(1)} %collective-permute-done.17.refs_14_), channel_id=1, source_target_pairs={{0,15},{1,0},{2,1},{3,2},{4,3},{5,4},{6,5},{7,6},{8,7},{9,8},{10,9... | collective-permute-start | bytes 798728 | tf_op jit(solution)/shard_map/ppermute | solution.py:135
  64.4 1.9 %collective-permute-start.20 = (bf16[1040,128]{1,0:T(8,128)(2,1)S(1)}, bf16[1040,128]{1,0:T(8,128)(2,1)S(1)}, u32[]{:S(2)}, u32[]{:S(2)}) collective-permute-start(bf16[1040,128]{1,0:T(8,128)(2,1)S(1)} %collective-permute-done.18.refs_15_), channel_id=1, source_target_pairs={{0,256},{1,257},{2,258},{3,259},{4,260},{5,261},{6,262},{7,263},{8... | collective-permute-start | bytes 798728 | tf_op jit(solution)/shard_map/ppermute | solution.py:135
  66.4 3.4 %collective-permute-start.19 = (bf16[1040,128]{1,0:T(8,128)(2,1)S(1)}, bf16[1040,128]{1,0:T(8,128)(2,1)S(1)}, u32[]{:S(2)}, u32[]{:S(2)}) collective-permute-start(bf16[1040,128]{1,0:T(8,128)(2,1)S(1)} %collective-permute-done.17.refs_14_), channel_id=1, source_target_pairs={{0,256},{1,257},{2,258},{3,259},{4,260},{5,261},{6,262},{7,263},{8... | collective-permute-start | bytes 798728 | tf_op jit(solution)/shard_map/ppermute | solution.py:135
  69.8 1.9 %collective-permute-start.24 = (bf16[1040,128]{1,0:T(8,128)(2,1)S(1)}, bf16[1040,128]{1,0:T(8,128)(2,1)S(1)}, u32[]{:S(2)}, u32[]{:S(2)}) collective-permute-start(bf16[1040,128]{1,0:T(8,128)(2,1)S(1)} %collective-permute-done.22.refs_19_), channel_id=1, source_target_pairs={{0,256},{1,257},{2,258},{3,259},{4,260},{5,261},{6,262},{7,263},{8... | collective-permute-start | bytes 798728 | tf_op jit(solution)/shard_map/ppermute | solution.py:135
  71.7 3.4 %collective-permute-start.23 = (bf16[1040,128]{1,0:T(8,128)(2,1)S(1)}, bf16[1040,128]{1,0:T(8,128)(2,1)S(1)}, u32[]{:S(2)}, u32[]{:S(2)}) collective-permute-start(bf16[1040,128]{1,0:T(8,128)(2,1)S(1)} %collective-permute-done.21.refs_18_), channel_id=1, source_target_pairs={{0,256},{1,257},{2,258},{3,259},{4,260},{5,261},{6,262},{7,263},{8... | collective-permute-start | bytes 798728 | tf_op jit(solution)/shard_map/ppermute | solution.py:135
  75.1 2.1 %collective-permute-start.6 = (bf16[1040,128]{1,0:T(8,128)(2,1)S(1)}, bf16[1040,128]{1,0:T(8,128)(2,1)}, u32[]{:S(2)}, u32[]{:S(2)}) collective-permute-start(bf16[1040,128]{1,0:T(8,128)(2,1)S(1)} %slice_bitcast_fusion.3), channel_id=1, source_target_pairs={{0,192},{1,193},{2,194},{3,195},{4,196},{5,197},{6,198},{7,199},{8... | collective-permute-start | bytes 798728 | tf_op jit(solution)/shard_map/ppermute | solution.py:135
  77.9 9.6 %collective-permute-start.8 = (bf16[2,1040,128]{2,1,0:T(8,128)(2,1)S(1)}, bf16[2,1040,128]{2,1,0:T(8,128)(2,1)}, u32[]{:S(2)}, u32[]{:S(2)}) collective-permute-start(bf16[2,1040,128]{2,1,0:T(8,128)(2,1)S(1)} %pad_maximum_fusion.refs_0_), channel_id=1, source_target_pairs={{0,16},{1,17},{2,18},{3,19},{4,20},{5,21},{6,22},{7,23},{8,24},{9,... | collective-permute-start | bytes 1597448 | tf_op jit(solution)/shard_map/ppermute | solution.py:135
  88.3 3.6 %collective-permute-start.7 = (bf16[1040,128]{1,0:T(8,128)(2,1)S(1)}, bf16[1040,128]{1,0:T(8,128)(2,1)}, u32[]{:S(2)}, u32[]{:S(2)}) collective-permute-start(bf16[1040,128]{1,0:T(8,128)(2,1)S(1)} %slice_bitcast_fusion.2), channel_id=1, source_target_pairs={{0,64},{1,65},{2,66},{3,67},{4,68},{5,69},{6,70},{7,71},{8,72},{9,... | collective-permute-start | bytes 798728 | tf_op jit(solution)/shard_map/ppermute | solution.py:135
  92.6 2.2 %collective-permute-start.10 = (bf16[2,1040,128]{2,1,0:T(8,128)(2,1)S(1)}, bf16[2,1040,128]{2,1,0:T(8,128)(2,1)}, u32[]{:S(2)}, u32[]{:S(2)}) collective-permute-start(bf16[2,1040,128]{2,1,0:T(8,128)(2,1)S(1)} %collective-permute-done.5.refs_2_), channel_id=1, source_target_pairs={{0,16},{1,17},{2,18},{3,19},{4,20},{5,21},{6,22},{7,23},{8,24},{9,... | collective-permute-start | bytes 1597448 | tf_op jit(solution)/shard_map/ppermute | solution.py:135
  95.5 2.1 %collective-permute-start.9 = (bf16[2,1040,128]{2,1,0:T(8,128)(2,1)S(1)}, bf16[2,1040,128]{2,1,0:T(8,128)(2,1)}, u32[]{:S(2)}, u32[]{:S(2)}) collective-permute-start(bf16[2,1040,128]{2,1,0:T(8,128)(2,1)S(1)} %collective-permute-done.4.refs_1_), channel_id=1, source_target_pairs={{0,16},{1,17},{2,18},{3,19},{4,20},{5,21},{6,22},{7,23},{8,24},{9,... | collective-permute-start | bytes 1597448 | tf_op jit(solution)/shard_map/ppermute | solution.py:135
  97.6 2.2 %collective-permute-start.11 = (bf16[1,1040,128]{2,1,0:T(8,128)(2,1)}, bf16[1,1040,128]{2,1,0:T(8,128)(2,1)}, u32[]{:S(2)}, u32[]{:S(2)}) collective-permute-start(bf16[1,1040,128]{2,1,0:T(8,128)(2,1)} %bitcast.35.refs_3_), channel_id=1, source_target_pairs={{0,16},{1,17},{2,18},{3,19},{4,20},{5,21},{6,22},{7,23},{8,24},{9,... | collective-permute-start | bytes 798728 | tf_op jit(solution)/shard_map/ppermute | solution.py:135
  99.9 2.3 %collective-permute-start.12 = (bf16[1,1040,128]{2,1,0:T(8,128)(2,1)}, bf16[1,1040,128]{2,1,0:T(8,128)(2,1)}, u32[]{:S(2)}, u32[]{:S(2)}) collective-permute-start(bf16[1,1040,128]{2,1,0:T(8,128)(2,1)} %bitcast.37.refs_4_), channel_id=1, source_target_pairs={{0,16},{1,17},{2,18},{3,19},{4,20},{5,21},{6,22},{7,23},{8,24},{9,... | collective-permute-start | bytes 798728 | tf_op jit(solution)/shard_map/ppermute | solution.py:135
  103.7 1.0 copy-done.1
  104.6 0.9 copy-done.3
  105.6 0.9 copy-done.5
  108.4 19.4 %shard_map.28 = f32[16,128,128]{2,1,0:T(8,128)} custom-call(s32[128]{0:T(128)S(1)} %get-tuple-element.11.own_table, s32[32]{0:T(128)S(1)} %bitcast_select_fusion.own_cells, s32[21]{0:T(128)S(1)} %stack.96.meta, bf16[4096,128]{1,0:T(8,128)(2,1)} %bitcast.62, bf16[2,1040,128]{2,1,0:T(8,128)(2,1)S(1)} %pad_maximum_fusion.refs_0_, ...), custom_call_target="tpu_custom_call" | custom-call | tf_op jit(solution)/shard_map/pallas_call | solution.py:175
  (59 shorter events, 8.0 us)
Async XLA Ops:
  0.0 11.2 %copy-start.10 = (bf16[1,1,32,128,128]{4,3,2,1,0:T(8,128)(2,1)S(1)}, bf16[1,1,32,128,128]{4,3,2,1,0:T(8,128)(2,1)}, u32[]{:S(2)}) copy-start(bf16[1,1,32,128,128]{4,3,2,1,0:T(8,128)(2,1)} %param.2) | copy-start | bytes 3145732
  3.7 7.6 %collective-permute-start.2 = (bf16[1040,128]{1,0:T(8,128)(2,1)S(1)}, bf16[1040,128]{1,0:T(8,128)(2,1)S(1)}, u32[]{:S(2)}, u32[]{:S(2)}) collective-permute-start(bf16[1040,128]{1,0:T(8,128)(2,1)S(1)} %get-tuple-element.5), channel_id=1, source_target_pairs={{0,64},{13,77},{14,78},{15,79},{16,80},{17,81},{30,94},{31,95},{32... | collective-permute-start | bytes 798728 | tf_op jit(solution)/shard_map/ppermute | solution.py:135
  7.7 5.5 %collective-permute-start = (bf16[1040,128]{1,0:T(8,128)(2,1)S(1)}, bf16[1040,128]{1,0:T(8,128)(2,1)S(1)}, u32[]{:S(2)}, u32[]{:S(2)}) collective-permute-start(bf16[1040,128]{1,0:T(8,128)(2,1)S(1)} %get-tuple-element.6), channel_id=1, source_target_pairs={{0,192},{13,205},{14,206},{15,207},{16,208},{17,209},{30,222},{31,... | collective-permute-start | bytes 798728 | tf_op jit(solution)/shard_map/ppermute | solution.py:135
  9.9 6.6 %collective-permute-start.1 = (bf16[1040,128]{1,0:T(8,128)(2,1)S(1)}, bf16[1040,128]{1,0:T(8,128)(2,1)S(1)}, u32[]{:S(2)}, u32[]{:S(2)}) collective-permute-start(bf16[1040,128]{1,0:T(8,128)(2,1)S(1)} %get-tuple-element.7), channel_id=1, source_target_pairs={{0,128},{13,141},{14,142},{15,143},{16,144},{17,145},{30,158},{31,... | collective-permute-start | bytes 798728 | tf_op jit(solution)/shard_map/ppermute | solution.py:135
  16.6 17.7 %collective-permute-start.3 = (bf16[1040,128]{1,0:T(8,128)(2,1)S(1)}, bf16[1040,128]{1,0:T(8,128)(2,1)S(1)}, u32[]{:S(2)}, u32[]{:S(2)}) collective-permute-start(bf16[1040,128]{1,0:T(8,128)(2,1)S(1)} %fusion.8), channel_id=1, source_target_pairs={{0,288},{1,289},{2,290},{3,291},{4,292},{5,293},{6,294},{7,295},{8... | collective-permute-start | bytes 798728 | tf_op jit(solution)/shard_map/ppermute | solution.py:135
  23.1 18.5 %collective-permute-start.14 = (bf16[1040,128]{1,0:T(8,128)(2,1)S(1)}, bf16[1040,128]{1,0:T(8,128)(2,1)S(1)}, u32[]{:S(2)}, u32[]{:S(2)}) collective-permute-start(bf16[1040,128]{1,0:T(8,128)(2,1)S(1)} %get-tuple-element.8), channel_id=1, source_target_pairs={{0,15},{1,0},{2,1},{3,2},{4,3},{5,4},{6,5},{7,6},{8,7},{9,8},{10,9... | collective-permute-start | bytes 798728 | tf_op jit(solution)/shard_map/ppermute | solution.py:135
  31.7 12.5 %collective-permute-start.13 = (bf16[1040,128]{1,0:T(8,128)(2,1)S(1)}, bf16[1040,128]{1,0:T(8,128)(2,1)S(1)}, u32[]{:S(2)}, u32[]{:S(2)}) collective-permute-start(bf16[1040,128]{1,0:T(8,128)(2,1)S(1)} %get-tuple-element.9), channel_id=1, source_target_pairs={{0,15},{1,0},{2,1},{3,2},{4,3},{5,4},{6,5},{7,6},{8,7},{9,8},{10,9... | collective-permute-start | bytes 798728 | tf_op jit(solution)/shard_map/ppermute | solution.py:135
  34.4 68.9 %copy-start.11 = (s32[1,1,2,32]{3,2,1,0:T(2,128)S(1)}, s32[1,1,2,32]{3,2,1,0:T(2,128)}, u32[]{:S(2)}) copy-start(s32[1,1,2,32]{3,2,1,0:T(2,128)} %param.3) | copy-start | bytes 772
  34.5 27.3 %collective-permute-start.5 = (bf16[2,1040,128]{2,1,0:T(8,128)(2,1)S(1)}, bf16[2,1040,128]{2,1,0:T(8,128)(2,1)S(1)}, u32[]{:S(2)}, u32[]{:S(2)}) collective-permute-start(bf16[2,1040,128]{2,1,0:T(8,128)(2,1)S(1)} %pad_maximum_fusion.refs_0_), channel_id=1, source_target_pairs={{0,192},{1,193},{2,194},{3,195},{4,196},{5,197},{6,198},{7,199},{8... | collective-permute-start | bytes 1597448 | tf_op jit(solution)/shard_map/ppermute | solution.py:135
  41.5 12.7 %collective-permute-start.18 = (bf16[1040,128]{1,0:T(8,128)(2,1)S(1)}, bf16[1040,128]{1,0:T(8,128)(2,1)S(1)}, u32[]{:S(2)}, u32[]{:S(2)}) collective-permute-start(bf16[1040,128]{1,0:T(8,128)(2,1)S(1)} %collective-permute-done.14.refs_11_), channel_id=1, source_target_pairs={{0,15},{1,0},{2,1},{3,2},{4,3},{5,4},{6,5},{7,6},{8,7},{9,8},{10,9... | collective-permute-start | bytes 798728 | tf_op jit(solution)/shard_map/ppermute | solution.py:135
  44.2 13.4 %collective-permute-start.17 = (bf16[1040,128]{1,0:T(8,128)(2,1)S(1)}, bf16[1040,128]{1,0:T(8,128)(2,1)S(1)}, u32[]{:S(2)}, u32[]{:S(2)}) collective-permute-start(bf16[1040,128]{1,0:T(8,128)(2,1)S(1)} %collective-permute-done.13.refs_10_), channel_id=1, source_target_pairs={{0,15},{1,0},{2,1},{3,2},{4,3},{5,4},{6,5},{7,6},{8,7},{9,8},{10,9... | collective-permute-start | bytes 798728 | tf_op jit(solution)/shard_map/ppermute | solution.py:135
  46.9 24.8 %collective-permute-start.4 = (bf16[2,1040,128]{2,1,0:T(8,128)(2,1)S(1)}, bf16[2,1040,128]{2,1,0:T(8,128)(2,1)S(1)}, u32[]{:S(2)}, u32[]{:S(2)}) collective-permute-start(bf16[2,1040,128]{2,1,0:T(8,128)(2,1)S(1)} %pad_maximum_fusion.refs_0_), channel_id=1, source_target_pairs={{0,64},{1,65},{2,66},{3,67},{4,68},{5,69},{6,70},{7,71},{8,72},{9,... | collective-permute-start | bytes 1597448 | tf_op jit(solution)/shard_map/ppermute | solution.py:135
  52.3 12.1 %collective-permute-start.16 = (bf16[1040,128]{1,0:T(8,128)(2,1)S(1)}, bf16[1040,128]{1,0:T(8,128)(2,1)S(1)}, u32[]{:S(2)}, u32[]{:S(2)}) collective-permute-start(bf16[1040,128]{1,0:T(8,128)(2,1)S(1)} %collective-permute-done.14.refs_11_), channel_id=1, source_target_pairs={{0,256},{1,257},{2,258},{3,259},{4,260},{5,261},{6,262},{7,263},{8... | collective-permute-start | bytes 798728 | tf_op jit(solution)/shard_map/ppermute | solution.py:135
  54.2 20.9 %collective-permute-start.15 = (bf16[1040,128]{1,0:T(8,128)(2,1)S(1)}, bf16[1040,128]{1,0:T(8,128)(2,1)S(1)}, u32[]{:S(2)}, u32[]{:S(2)}) collective-permute-start(bf16[1040,128]{1,0:T(8,128)(2,1)S(1)} %collective-permute-done.13.refs_10_), channel_id=1, source_target_pairs={{0,256},{1,257},{2,258},{3,259},{4,260},{5,261},{6,262},{7,263},{8... | collective-permute-start | bytes 798728 | tf_op jit(solution)/shard_map/ppermute | solution.py:135
  57.6 8.7 %collective-permute-start.22 = (bf16[1040,128]{1,0:T(8,128)(2,1)S(1)}, bf16[1040,128]{1,0:T(8,128)(2,1)S(1)}, u32[]{:S(2)}, u32[]{:S(2)}) collective-permute-start(bf16[1040,128]{1,0:T(8,128)(2,1)S(1)} %collective-permute-done.18.refs_15_), channel_id=1, source_target_pairs={{0,15},{1,0},{2,1},{3,2},{4,3},{5,4},{6,5},{7,6},{8,7},{9,8},{10,9... | collective-permute-start | bytes 798728 | tf_op jit(solution)/shard_map/ppermute | solution.py:135
  61.7 8.0 %collective-permute-start.21 = (bf16[1040,128]{1,0:T(8,128)(2,1)S(1)}, bf16[1040,128]{1,0:T(8,128)(2,1)S(1)}, u32[]{:S(2)}, u32[]{:S(2)}) collective-permute-start(bf16[1040,128]{1,0:T(8,128)(2,1)S(1)} %collective-permute-done.17.refs_14_), channel_id=1, source_target_pairs={{0,15},{1,0},{2,1},{3,2},{4,3},{5,4},{6,5},{7,6},{8,7},{9,8},{10,9... | collective-permute-start | bytes 798728 | tf_op jit(solution)/shard_map/ppermute | solution.py:135
  64.4 12.8 %collective-permute-start.20 = (bf16[1040,128]{1,0:T(8,128)(2,1)S(1)}, bf16[1040,128]{1,0:T(8,128)(2,1)S(1)}, u32[]{:S(2)}, u32[]{:S(2)}) collective-permute-start(bf16[1040,128]{1,0:T(8,128)(2,1)S(1)} %collective-permute-done.18.refs_15_), channel_id=1, source_target_pairs={{0,256},{1,257},{2,258},{3,259},{4,260},{5,261},{6,262},{7,263},{8... | collective-permute-start | bytes 798728 | tf_op jit(solution)/shard_map/ppermute | solution.py:135
  66.4 21.2 %collective-permute-start.19 = (bf16[1040,128]{1,0:T(8,128)(2,1)S(1)}, bf16[1040,128]{1,0:T(8,128)(2,1)S(1)}, u32[]{:S(2)}, u32[]{:S(2)}) collective-permute-start(bf16[1040,128]{1,0:T(8,128)(2,1)S(1)} %collective-permute-done.17.refs_14_), channel_id=1, source_target_pairs={{0,256},{1,257},{2,258},{3,259},{4,260},{5,261},{6,262},{7,263},{8... | collective-permute-start | bytes 798728 | tf_op jit(solution)/shard_map/ppermute | solution.py:135
  69.7 25.0 %copy-start = (bf16[1040,128]{1,0:T(8,128)(2,1)}, bf16[1040,128]{1,0:T(8,128)(2,1)S(1)}, u32[]{:S(2)}) copy-start(bf16[1040,128]{1,0:T(8,128)(2,1)S(1)} %collective-permute-done.21.refs_18_) | copy-start | bytes 798724
  69.8 22.1 %collective-permute-start.24 = (bf16[1040,128]{1,0:T(8,128)(2,1)S(1)}, bf16[1040,128]{1,0:T(8,128)(2,1)S(1)}, u32[]{:S(2)}, u32[]{:S(2)}) collective-permute-start(bf16[1040,128]{1,0:T(8,128)(2,1)S(1)} %collective-permute-done.22.refs_19_), channel_id=1, source_target_pairs={{0,256},{1,257},{2,258},{3,259},{4,260},{5,261},{6,262},{7,263},{8... | collective-permute-start | bytes 798728 | tf_op jit(solution)/shard_map/ppermute | solution.py:135
  71.7 23.1 %collective-permute-start.23 = (bf16[1040,128]{1,0:T(8,128)(2,1)S(1)}, bf16[1040,128]{1,0:T(8,128)(2,1)S(1)}, u32[]{:S(2)}, u32[]{:S(2)}) collective-permute-start(bf16[1040,128]{1,0:T(8,128)(2,1)S(1)} %collective-permute-done.21.refs_18_), channel_id=1, source_target_pairs={{0,256},{1,257},{2,258},{3,259},{4,260},{5,261},{6,262},{7,263},{8... | collective-permute-start | bytes 798728 | tf_op jit(solution)/shard_map/ppermute | solution.py:135
  75.1 22.5 %collective-permute-start.6 = (bf16[1040,128]{1,0:T(8,128)(2,1)S(1)}, bf16[1040,128]{1,0:T(8,128)(2,1)}, u32[]{:S(2)}, u32[]{:S(2)}) collective-permute-start(bf16[1040,128]{1,0:T(8,128)(2,1)S(1)} %slice_bitcast_fusion.3), channel_id=1, source_target_pairs={{0,192},{1,193},{2,194},{3,195},{4,196},{5,197},{6,198},{7,199},{8... | collective-permute-start | bytes 798728 | tf_op jit(solution)/shard_map/ppermute | solution.py:135
  77.9 25.4 %collective-permute-start.8 = (bf16[2,1040,128]{2,1,0:T(8,128)(2,1)S(1)}, bf16[2,1040,128]{2,1,0:T(8,128)(2,1)}, u32[]{:S(2)}, u32[]{:S(2)}) collective-permute-start(bf16[2,1040,128]{2,1,0:T(8,128)(2,1)S(1)} %pad_maximum_fusion.refs_0_), channel_id=1, source_target_pairs={{0,16},{1,17},{2,18},{3,19},{4,20},{5,21},{6,22},{7,23},{8,24},{9,... | collective-permute-start | bytes 1597448 | tf_op jit(solution)/shard_map/ppermute | solution.py:135
  88.3 11.6 %collective-permute-start.7 = (bf16[1040,128]{1,0:T(8,128)(2,1)S(1)}, bf16[1040,128]{1,0:T(8,128)(2,1)}, u32[]{:S(2)}, u32[]{:S(2)}) collective-permute-start(bf16[1040,128]{1,0:T(8,128)(2,1)S(1)} %slice_bitcast_fusion.2), channel_id=1, source_target_pairs={{0,64},{1,65},{2,66},{3,67},{4,68},{5,69},{6,70},{7,71},{8,72},{9,... | collective-permute-start | bytes 798728 | tf_op jit(solution)/shard_map/ppermute | solution.py:135
  92.6 11.1 %collective-permute-start.10 = (bf16[2,1040,128]{2,1,0:T(8,128)(2,1)S(1)}, bf16[2,1040,128]{2,1,0:T(8,128)(2,1)}, u32[]{:S(2)}, u32[]{:S(2)}) collective-permute-start(bf16[2,1040,128]{2,1,0:T(8,128)(2,1)S(1)} %collective-permute-done.5.refs_2_), channel_id=1, source_target_pairs={{0,16},{1,17},{2,18},{3,19},{4,20},{5,21},{6,22},{7,23},{8,24},{9,... | collective-permute-start | bytes 1597448 | tf_op jit(solution)/shard_map/ppermute | solution.py:135
  95.5 8.2 %collective-permute-start.9 = (bf16[2,1040,128]{2,1,0:T(8,128)(2,1)S(1)}, bf16[2,1040,128]{2,1,0:T(8,128)(2,1)}, u32[]{:S(2)}, u32[]{:S(2)}) collective-permute-start(bf16[2,1040,128]{2,1,0:T(8,128)(2,1)S(1)} %collective-permute-done.4.refs_1_), channel_id=1, source_target_pairs={{0,16},{1,17},{2,18},{3,19},{4,20},{5,21},{6,22},{7,23},{8,24},{9,... | collective-permute-start | bytes 1597448 | tf_op jit(solution)/shard_map/ppermute | solution.py:135
  97.6 5.7 %collective-permute-start.11 = (bf16[1,1040,128]{2,1,0:T(8,128)(2,1)}, bf16[1,1040,128]{2,1,0:T(8,128)(2,1)}, u32[]{:S(2)}, u32[]{:S(2)}) collective-permute-start(bf16[1,1040,128]{2,1,0:T(8,128)(2,1)} %bitcast.35.refs_3_), channel_id=1, source_target_pairs={{0,16},{1,17},{2,18},{3,19},{4,20},{5,21},{6,22},{7,23},{8,24},{9,... | collective-permute-start | bytes 798728 | tf_op jit(solution)/shard_map/ppermute | solution.py:135
  99.9 3.8 %collective-permute-start.12 = (bf16[1,1040,128]{2,1,0:T(8,128)(2,1)}, bf16[1,1040,128]{2,1,0:T(8,128)(2,1)}, u32[]{:S(2)}, u32[]{:S(2)}) collective-permute-start(bf16[1,1040,128]{2,1,0:T(8,128)(2,1)} %bitcast.37.refs_4_), channel_id=1, source_target_pairs={{0,16},{1,17},{2,18},{3,19},{4,20},{5,21},{6,22},{7,23},{8,24},{9,... | collective-permute-start | bytes 798728 | tf_op jit(solution)/shard_map/ppermute | solution.py:135
  103.7 1.0 copy-start.1
  104.6 1.0 copy-start.3
  105.6 1.0 copy-start.5
  106.5 1.0 copy-start.7
  (5 other events, 3.7 us)

commit v2 on v0

v2 whole, which is shorter than its diff:
```python
import functools

import jax
import jax.numpy as jnp
from jax import lax
from jax.experimental import pallas as pl
from jax.experimental.pallas import tpu as pltpu
from jax.sharding import PartitionSpec as P

H = 8
STEPS = 4
W = 128
HEAD = 16
TILE = 32 * W
HALF = TILE // 2
LONG = HALF + HEAD
PACK = TILE + HEAD
DENSE = H * W
AXES = ("layer", "row", "col")
BF = jnp.bfloat16


def pairs_of(mesh_shape, target):
    layers, rows, cols = mesh_shape
    flat = lambda at: (at[0] * rows + at[1]) * cols + at[2]
    found = []
    for l in range(layers):
        for r in range(rows):
            for c in range(cols):
                to = target(l, r, c)
                if to is not None:
                    found.append((flat((l, r, c)), flat(to)))
    return found


def is_relay(l, r):
    return r % 2 == l


def from_root(r, c):
    return ((r - c) // 4) % 4


def cells_and_table(coords):
    slots = coords.shape[1]
    values = jnp.arange(W, dtype=jnp.int32)
    used = jnp.any(coords[:, :, None] == values[None, None, :], axis=1)
    below = used[:, None, :] & (values[None, None, :] < coords[:, :, None])
    rank = jnp.sum(below.astype(jnp.int32), axis=2)
    cells = jnp.where(coords[0] >= 0, rank[0] * H + rank[1], H * H)
    hits = cells[None, :] == values[:, None]
    order = jnp.arange(slots, dtype=jnp.int32) - slots
    table = slots + jnp.sum(jnp.where(hits, order[None, :], 0), axis=1)
    return cells, table


class Loads:
    def __init__(self, sems):
        self.sems, self.count = sems, 0

    def start(self, choices, dst):
        sem = self.sems.at[self.count]
        self.count += 1
        for holds, src in choices:
            if holds is None:
                pltpu.make_async_copy(src, dst, sem).start()
            else:
                @pl.when(holds)
                def _():
                    pltpu.make_async_copy(src, dst, sem).start()
        src = choices[0][1]
        return lambda: pltpu.make_async_copy(src, dst, sem).wait()


def load_tile(loads, choices, tiles, heads, at, head_at):
    return [
        loads.start([(h, src.at[pl.ds(0, TILE)]) for h, src in choices], tiles.at[at, pl.ds(0, TILE)]),
        loads.start([(h, src.at[pl.ds(TILE, HEAD)]) for h, src in choices], heads.at[head_at]),
    ]


def read_tables(own_table, heads, table_v, table_s, sem):
    for i, head in enumerate(heads):
        if head is None:
            table_v[i:i + 1, :] = jnp.zeros((1, W), jnp.int32)
        else:
            table_v[i:i + 1, :] = head[0:1, :].astype(jnp.float32).astype(jnp.int32)
    copy = pltpu.make_async_copy(table_v, table_s, sem)
    copy.start()
    copy.wait()
    for i, head in enumerate(heads):
        if head is None:
            @pl.loop(0, H * H)
            def _(j):
                table_s[i, j] = own_table[j]


def add_product(a_ref, b_ref, a_row, b_row, table_s, cells, base, out):
    def block_of(ref, at, cell):
        return ref[pl.ds(pl.multiple_of(table_s[at, cell] * W, W), W), :]

    @pl.loop(0, 16, unroll=2)
    def _(q):
        cell = cells[base + q]
        held = jnp.minimum(cell, H * H - 1)
        r, c = held // H, held % H
        left = jnp.concatenate([block_of(a_ref, a_row, r * H + k) for k in range(H)], axis=1)
        right = jnp.concatenate([block_of(b_ref, b_row, k * H + c) for k in range(H)], axis=0)
        block = jnp.dot(left, right, preferred_element_type=jnp.float32)
        out[q] += jnp.where(cell < H * H, block, jnp.zeros_like(block))


def some_kernel(count, first, own_table, cells, meta, own, *refs):
    before, refs = (None, refs) if first == 0 else (refs[0], refs[1:])
    lefts, (b1r, b1s, b2r, b2s), refs = refs[:count], refs[count:count + 4], refs[count + 4:]
    out, a_all, b_all, heads, table_v, table_s, sems = refs
    relay = meta[0] == 1
    spread = meta[0] == 0
    loads = Loads(sems)
    waits = [loads.start([(None, own)], b_all.at[0, pl.ds(0, TILE)])]
    for i, src in enumerate(lefts):
        waits += load_tile(loads, [(None, src)], a_all, heads, i, 2 + i)
    for s, (on_relay, on_spread) in enumerate(((b1r, b1s), (b2r, b2s)), 1):
        waits += load_tile(loads, [(spread, on_spread), (relay, on_relay)], b_all, heads, s, s - 1)
    for i in range(count):
        a_all[i, TILE:, :] = jnp.zeros((W, W), BF)
    for i in range(3):
        b_all[i, TILE:, :] = jnp.zeros((W, W), BF)
    out[...] = jnp.zeros_like(out) if before is None else before[...]
    for wait in waits:
        wait()
    rows = [None] + [heads.at[i] for i in range(2 + count)]
    read_tables(own_table, rows, table_v, table_s, sems.at[loads.count])

    @pl.loop(0, count)
    def _(i):
        step = meta[1 + first + i]

        @pl.when(step < 3)
        def _():
            add_product(a_all.at[i], b_all.at[step], 3 + i, step, table_s, cells, meta[5], out)


def late_kernel(own_table, cells, meta, own, before, t0, t1, t2, t3, b1r, b1s, b2r, b2s, b3r, b3s,
                out, a_all, b_all, heads, table_v, table_s, sems):
    relay = meta[0] == 1
    spread = meta[0] == 0
    far_step = meta[4]
    loads = Loads(sems)
    waits = load_tile(loads, [(None, t3)], a_all, heads, 0, 0)
    choices = []
    for i, src in enumerate((t0, t1, t2)):
        holds = meta[1 + i] == 3
        choices.append((jnp.logical_or(holds, far_step == 3) if i == 0 else holds, src))
    waits += load_tile(loads, choices, a_all, heads, 1, 1)
    waits += load_tile(loads, [(spread, b3s), (relay, b3r)], b_all, heads, 1, 3)
    tiles, tops = [(far_step == 0, own)], [(far_step == 0, b1r.at[pl.ds(TILE, HEAD)])]
    for s, (on_relay, on_spread) in enumerate(((b1r, b1s), (b2r, b2s), (b3r, b3s)), 1):
        for role, src in ((relay, on_relay), (spread, on_spread)):
            holds = jnp.logical_and(role, far_step == s)
            tiles.append((holds, src.at[pl.ds(0, TILE)]))
            tops.append((holds, src.at[pl.ds(TILE, HEAD)]))
    waits.append(loads.start(tiles, b_all.at[0, pl.ds(0, TILE)]))
    waits.append(loads.start(tops, heads.at[2]))
    for i in range(2):
        a_all[i, TILE:, :] = jnp.zeros((W, W), BF)
        b_all[i, TILE:, :] = jnp.zeros((W, W), BF)
    out[...] = before[...]
    for wait in waits:
        wait()
    read_tables(own_table, [heads.at[0], heads.at[1], heads.at[2], heads.at[3], None], table_v, table_s, sems.at[loads.count])

    @pl.loop(0, 2)
    def _(i):
        @pl.when((i == 0) | (far_step < 3))
        def _():
            b_row = jnp.where((i == 0) & (far_step == 0), 4, 2 + i)
            add_product(a_all.at[i], b_all.at[i], i, b_row, table_s, cells, meta[5], out)


def call(kernel, lefts, rights, us, smem_ops, vmem_ops, any_ops):
    smem = pl.BlockSpec(memory_space=pltpu.SMEM)
    vmem = pl.BlockSpec(memory_space=pltpu.VMEM)
    anywhere = pl.BlockSpec(memory_space=pl.ANY)
    return pl.pallas_call(
        kernel,
        out_shape=jax.ShapeDtypeStruct((16, W, W), jnp.float32),
        in_specs=[smem] * len(smem_ops) + [anywhere] + [vmem] * len(vmem_ops) + [anywhere] * (len(any_ops) - 1),
        out_specs=vmem,
        scratch_shapes=[
            pltpu.VMEM((lefts, TILE + W, W), BF),
            pltpu.VMEM((rights, TILE + W, W), BF),
            pltpu.VMEM((5, HEAD, W), BF),
            pltpu.VMEM((8, W), jnp.int32),
            pltpu.SMEM((8, W), jnp.int32),
            pltpu.SemaphoreType.DMA((24,)),
        ],
        compiler_params=pltpu.CompilerParams(vmem_limit_bytes=24 * 1024 * 1024),
        cost_estimate=pl.CostEstimate(flops=int(us * 1.15e9), bytes_accessed=0, transcendentals=0),
    )(*smem_ops, any_ops[0], *vmem_ops, *any_ops[1:])


def body(mesh_shape, x_blocks, x_coords):
    tile = x_blocks.reshape(TILE, W)
    coords = x_coords[0, 0]
    rows, cols = mesh_shape[1:]
    layer, row, col = (lax.axis_index(a) for a in AXES)

    def send(value, target):
        return lax.ppermute(value, AXES, pairs_of(mesh_shape, target))

    def after(value, *others):
        return lax.optimization_barrier((value, *others))[0]

    cells, table = cells_and_table(coords)
    head = jnp.broadcast_to(table.astype(BF)[None, :], (HEAD, W))
    full = after(jnp.concatenate([tile, head]))

    low = after(tile[:LONG])
    high = after(full[HALF:])

    down = lambda l, r, c: (l, r, (c - 1) % cols) if is_relay(l, r) else None
    over = lambda l, r, c: (1 - l, r, c) if is_relay(l, r) else None
    twin = lambda l, r, c: (l, r ^ 1, c)
    cross = lambda l, r, c: (1 - l, r ^ 2, c)

    def y_hop(starts, by):
        return lambda l, r, c: (l, (r + 4 * by) % rows, c) if from_root(r, c) in starts else None

    away = from_root(row, col)
    z1 = send(full, down)
    up1 = send(low, y_hop((0,), 1))
    dn1 = send(high, y_hop((0,), -1))
    x1 = send(z1, over)
    up2 = send(jnp.where(away == 0, high, up1), y_hop((0, 1), 1))
    dn2 = send(jnp.where(away == 0, low, dn1), y_hop((0, 3), -1))
    z2 = send(z1, down)
    first = jnp.where(away == 0, low, jnp.where(away == 1, up1, jnp.where(away == 2, up2, dn2)))
    second = jnp.where(away == 0, high, jnp.where(away == 1, up2, jnp.where(away == 2, dn2, dn1)))
    t0 = after(jnp.concatenate([first[:HALF], second]))
    t2 = send(t0, cross)
    t1 = send(t0, twin)
    z3 = send(after(z2, x1), down)
    x2 = send(z2, over)
    x3 = send(after(z3, x2), over)
    t3 = send(after(t2, t1), twin)

    steps = [((row ^ bit) - col) % 4 for bit in (0, 1, 2, 3)]
    meta = jnp.stack([(row % 2 == layer).astype(jnp.int32)] + steps + [16 * layer]).astype(jnp.int32)
    small = (table, cells, meta)
    near = (z1, x1, z2, x2)
    early = call(functools.partial(some_kernel, 2, 0), 2, 3, 20, small, (), (tile, t0, t1, *near))
    middle = call(functools.partial(some_kernel, 1, 2), 1, 3, 5, small, (early,), (tile, t2, *near))
    out = call(late_kernel, 2, 2, 10, small, (middle,), (tile, t0, t1, t2, t3, *near, z3, x3))
    return out[None, None]


def solution(mesh):
    return jax.shard_map(
        functools.partial(body, tuple(mesh.shape[a] for a in AXES)),
        mesh=mesh,
        in_specs=(P("col", "row", None, None, None), P("col", "row", None, None)),
        out_specs=P("col", "row", "layer", None, None),
        check_vma=False,
    )
```

time: 368 us -> 105 us (0.29)
  waiting for transfers between devices: 254 us -> 22.3 us
  local copies, waits for them, and re-layouts: 31.9 us -> 4.58 us
  starting transfers between devices: 24.4 us -> 48.8 us
  Pallas kernels: 0 us -> 21.4 us
  between operations: 13.7 us -> 0.18 us
  other arithmetic: 18.7 us -> 5.82 us
  blocking collectives: 12.8 us -> 0 us
  matrix products: 12 us -> 0 us
    psum x2 -> x0, waiting for transfers between devices: 212 us -> none  [the longest x1 126 us: broadcast(): return lax.psum(jnp.where(mine, shard, jnp.zeros_like(shard)), axis)]
    ppermute x4 -> x13, starting transfers between devices: 24.4 us -> 48.8 us  [send(): return lax.ppermute(value, AXES, pairs_of(mesh_shape, target))]
    pallas_call x0 -> x3, Pallas kernels: none -> 21.4 us  [call(): pl.pallas_call(kernel, out_shape=jax.ShapeDtypeStruct((16, W, W), jnp.flo...]
    ppermute x4 -> x13, waiting for transfers between devices: 41.7 us -> 22.3 us  [send(): return lax.ppermute(value, AXES, pairs_of(mesh_shape, target))]
    dot_general x4 -> x0, local copies, waits for them, and re-layouts: 14 us -> none  [tile_product(): whole = jnp.dot(left_grid, right_grid, preferred_element_type=jnp.float32)]
    gather x6 -> x0, local copies, waits for them, and re-layouts: 13.3 us -> none  [the longest x2 7.06 us: tile_product(): taken = cell_blocks[jnp.minimum(cells, H * H - 1)]]
    psum x1 -> x0, blocking collectives: 12.8 us -> none  [broadcast(): return lax.psum(jnp.where(mine, shard, jnp.zeros_like(shard)), axis)]
    dot_general x2 -> x0, matrix products: 12 us -> none  [tile_product(): whole = jnp.dot(left_grid, right_grid, preferred_element_type=jnp.float32)]
  transfers between devices with their start and end apart: 6 -> 13, of which waited for: 4 -> 5; matrix products, arithmetic and copies ran while one was open for 5% -> 7% of each run, Pallas kernels for 0% -> 12%
where the time goes in v2:
time: 105 us; the launch traced here: 103 us
  starting transfers between devices  48.8 us (46%)
  waiting for transfers between devices  22.3 us (21%)
  Pallas kernels  21.4 us (20%)
  other arithmetic  5.82 us (6%)
  local copies, waits for them, and re-layouts  4.58 us (4%)
    ppermute x13, starting transfers between devices, send(): return lax.ppermute(value, AXES, pairs_of(mesh_shape, target))  48.8 us
    ppermute x13, waiting for transfers between devices, send(): return lax.ppermute(value, AXES, pairs_of(mesh_shape, target))  22.3 us
    pallas_call x3, Pallas kernels, call(): pl.pallas_call(kernel, out_shape=jax.ShapeDtypeStruct((16, W, W), jnp.flo...  21.4 us
    unnamed x8, local copies, waits for them, and re-layouts  2.24 us
  transfers between devices with their start and end apart: 13, of which 5 were waited for; matrix products, arithmetic and copies ran while one was open for 7% of the time, Pallas kernels for 12%

profile of v2, /device:TPU:1, one launch (start us, length us, event | category | flops | bytes accessed | tf_op | source)
XLA Modules:
  0.0 103.0 jit_solution(16730322640914770842)
XLA Ops:
  0.0 1.2 %slice.25 = bf16[2064,128]{1,0:T(8,128)(2,1)S(1)} slice(bf16[4096,128]{1,0:T(8,128)(2,1)} %bitcast.19), slice={[0:2064], [0:128]} | slice | bytes 1056768 | tf_op jit(solution)/shard_map/slice | solution.py:219
  1.2 4.9 %collective-permute-start = (bf16[2064,128]{1,0:T(8,128)(2,1)S(1)}, bf16[2064,128]{1,0:T(8,128)(2,1)}, u32[]{:S(2)}, u32[]{:S(2)}) collective-permute-start(bf16[2064,128]{1,0:T(8,128)(2,1)S(1)} %slice.25), channel_id=1, source_target_pairs={{0,64},{13,77},{14,78},{15,79},{16,80},{17,81},{30,94},{31,95},{32... | collective-permute-start | bytes 1585160 | tf_op jit(solution)/shard_map/ppermute | solution.py:210
  6.1 0.1 fusion
  6.2 0.2 convert_reduce_fusion
  6.5 1.0 %pad_maximum_fusion = bf16[4112,128]{1,0:T(8,128)(2,1)} fusion(bf16[16,128]{1,0:T(8,128)(2,1)S(1)} %broadcast_in_dim.37, bf16[4096,128]{1,0:T(8,128)(2,1)S(1)} %bitcast.20), kind=kLoop, calls=%fused_computation | loop fusion | flops 2105344 | bytes 2105344 | tf_op jit(solution)/shard_map/concatenate | solution.py:217
  7.5 0.7 collective-permute-start.5
  8.3 1.1 %slice.26 = bf16[2064,128]{1,0:T(8,128)(2,1)S(1)} slice(bf16[4112,128]{1,0:T(8,128)(2,1)} %pad_maximum_fusion), slice={[2048:4112], [0:128]} | slice | bytes 1056768 | tf_op jit(solution)/shard_map/slice | solution.py:220
  9.3 2.9 %collective-permute-start.2 = (bf16[2064,128]{1,0:T(8,128)(2,1)S(1)}, bf16[2064,128]{1,0:T(8,128)(2,1)}, u32[]{:S(2)}, u32[]{:S(2)}) collective-permute-start(bf16[2064,128]{1,0:T(8,128)(2,1)S(1)} %slice.26), channel_id=1, source_target_pairs={{0,192},{13,205},{14,206},{15,207},{16,208},{17,209},{30,222},{31,... | collective-permute-start | bytes 1585160 | tf_op jit(solution)/shard_map/ppermute | solution.py:210
  12.3 0.4 collective-permute-done
  12.7 0.9 broadcast_select_fusion.1
  13.5 6.0 %collective-permute-start.1 = (bf16[2064,128]{1,0:T(8,128)(2,1)}, bf16[2064,128]{1,0:T(8,128)(2,1)}, u32[]{:S(2)}, u32[]{:S(2)}) collective-permute-start(bf16[2064,128]{1,0:T(8,128)(2,1)} %broadcast_select_fusion.1), channel_id=1, source_target_pairs={{0,64},{9,73},{10,74},{11,75},{12,76},{13,77},{14,78},{15,79},{16,... | collective-permute-start | bytes 1585160 | tf_op jit(solution)/shard_map/ppermute | solution.py:210
  19.6 0.9 broadcast_select_fusion
  20.4 5.0 %collective-permute-start.3 = (bf16[2064,128]{1,0:T(8,128)(2,1)}, bf16[2064,128]{1,0:T(8,128)(2,1)}, u32[]{:S(2)}, u32[]{:S(2)}) collective-permute-start(bf16[2064,128]{1,0:T(8,128)(2,1)} %broadcast_select_fusion), channel_id=1, source_target_pairs={{0,192},{1,193},{2,194},{3,195},{4,196},{13,205},{14,206},{15,207}... | collective-permute-start | bytes 1585160 | tf_op jit(solution)/shard_map/ppermute | solution.py:210
  25.4 1.6 %collective-permute-start.7 = (bf16[4112,128]{1,0:T(8,128)(2,1)S(1)}, bf16[4112,128]{1,0:T(8,128)(2,1)}, u32[]{:S(2)}, u32[]{:S(2)}) collective-permute-start(bf16[4112,128]{1,0:T(8,128)(2,1)S(1)} %collective-permute-done.5.refs_2_.b1r), channel_id=1, source_target_pairs={{0,15},{1,0},{2,1},{3,2},{4,3},{5,4},{6,5},{7,6},{8,7},{9,8},{10,9... | collective-permute-start | bytes 3158024 | tf_op jit(solution)/shard_map/ppermute | solution.py:210
  27.1 1.3 %collective-permute-start.6 = (bf16[4112,128]{1,0:T(8,128)(2,1)S(1)}, bf16[4112,128]{1,0:T(8,128)(2,1)S(1)}, u32[]{:S(2)}, u32[]{:S(2)}) collective-permute-start(bf16[4112,128]{1,0:T(8,128)(2,1)S(1)} %collective-permute-done.5.refs_2_.b1r), channel_id=1, source_target_pairs={{0,256},{1,257},{2,258},{3,259},{4,260},{5,261},{6,262},{7,263},{8... | collective-permute-start | bytes 3158024 | tf_op jit(solution)/shard_map/ppermute | solution.py:210
  28.4 6.8 %collective-permute-done.3 = bf16[2064,128]{1,0:T(8,128)(2,1)} collective-permute-done((bf16[2064,128]{1,0:T(8,128)(2,1)}, bf16[2064,128]{1,0:T(8,128)(2,1)}, u32[]{:S(2)}, u32[]{:S(2)}) %collective-permute-start.3) | collective-permute-done | bytes 528416 | tf_op jit(solution)/shard_map/ppermute | solution.py:210
  35.2 1.1 %select_select_fusion = bf16[2064,128]{1,0:T(8,128)(2,1)S(1)} fusion(bf16[2064,128]{1,0:T(8,128)(2,1)S(1)} %slice.26, bf16[2064,128]{1,0:T(8,128)(2,1)} %collective-permute-done.1, bf16[2064,128]{1,0:T(8,128)(2,1)} %collective-permute-done.3, bf16[2064,128]{1,0:T(8,128)(2,1)} %collective-permute-done.2, pred[]{:T(512)S(6)} %eq.68, pred[]{:T(512)S(6)} %eq.67, ...), kind=kLoop, calls=%fused_computation.2 | loop fusion | flops 792576 | bytes 2641923 | tf_op jit(solution)/shard_map/jit(_where)/select_n | solution.py:239
  36.3 1.5 %slice_select_fusion = bf16[2048,128]{1,0:T(8,128)(2,1)S(1)} fusion(bf16[2064,128]{1,0:T(8,128)(2,1)S(1)} %slice.25, bf16[2064,128]{1,0:T(8,128)(2,1)} %collective-permute-done, bf16[2064,128]{1,0:T(8,128)(2,1)} %collective-permute-done.3, bf16[2064,128]{1,0:T(8,128)(2,1)} %collective-permute-done.1, pred[]{:T(512)S(6)} %eq.66, pred[]{:T(512)S(6)} %eq.67, ...), kind=kLoop, calls=%fused_computation.5 | loop fusion | flops 786432 | bytes 2621443 | tf_op jit(solution)/shard_map/jit(_where)/select_n | solution.py:238
  37.9 13.6 %collective-permute-start.9 = (bf16[4112,128]{1,0:T(8,128)(2,1)S(1)}, bf16[4112,128]{1,0:T(8,128)(2,1)}, u32[]{:S(2)}, u32[]{:S(2)}) collective-permute-start(bf16[4112,128]{1,0:T(8,128)(2,1)S(1)} %pad_maximum_fusion.1.refs_0_.t0), channel_id=1, source_target_pairs={{0,288},{1,289},{2,290},{3,291},{4,292},{5,293},{6,294},{7,295},{8... | collective-permute-start | bytes 3158024 | tf_op jit(solution)/shard_map/ppermute | solution.py:210
  51.5 3.5 %collective-permute-start.4 = (bf16[4112,128]{1,0:T(8,128)(2,1)S(1)}, bf16[4112,128]{1,0:T(8,128)(2,1)}, u32[]{:S(2)}, u32[]{:S(2)}) collective-permute-start(bf16[4112,128]{1,0:T(8,128)(2,1)S(1)} %pad_maximum_fusion.1.refs_0_.t0), channel_id=1, source_target_pairs={{0,16},{1,17},{2,18},{3,19},{4,20},{5,21},{6,22},{7,23},{8,24},{9,... | collective-permute-start | bytes 3158024 | tf_op jit(solution)/shard_map/ppermute | solution.py:210
  55.0 3.5 %collective-permute-done.6.refs_3_.b1s = bf16[4112,128]{1,0:T(8,128)(2,1)S(1)} collective-permute-done((bf16[4112,128]{1,0:T(8,128)(2,1)S(1)}, bf16[4112,128]{1,0:T(8,128)(2,1)S(1)}, u32[]{:S(2)}, u32[]{:S(2)}) %collective-permute-start.6) | collective-permute-done | bytes 1052704 | tf_op jit(solution)/shard_map/ppermute | solution.py:210
  58.5 1.0 copy-done.1
  59.5 1.3 %collective-permute-start.8 = (bf16[4112,128]{1,0:T(8,128)(2,1)}, bf16[4112,128]{1,0:T(8,128)(2,1)}, u32[]{:S(2)}, u32[]{:S(2)}) collective-permute-start(bf16[4112,128]{1,0:T(8,128)(2,1)} %collective-permute-done.7.refs_4_.b2r), channel_id=1, source_target_pairs={{0,256},{1,257},{2,258},{3,259},{4,260},{5,261},{6,262},{7,263},{8... | collective-permute-start | bytes 3158024 | tf_op jit(solution)/shard_map/ppermute | solution.py:210
  60.8 1.6 %collective-permute-start.11 = (bf16[4112,128]{1,0:T(8,128)(2,1)}, bf16[4112,128]{1,0:T(8,128)(2,1)}, u32[]{:S(2)}, u32[]{:S(2)}) collective-permute-start(bf16[4112,128]{1,0:T(8,128)(2,1)} %collective-permute-done.7.refs_4_.b2r), channel_id=1, source_target_pairs={{0,15},{1,0},{2,1},{3,2},{4,3},{5,4},{6,5},{7,6},{8,7},{9,8},{10,9... | collective-permute-start | bytes 3158024 | tf_op jit(solution)/shard_map/ppermute | solution.py:210
  62.5 10.2 %collective-permute-done.9.refs_1_.t2 = bf16[4112,128]{1,0:T(8,128)(2,1)} collective-permute-done((bf16[4112,128]{1,0:T(8,128)(2,1)S(1)}, bf16[4112,128]{1,0:T(8,128)(2,1)}, u32[]{:S(2)}, u32[]{:S(2)}) %collective-permute-start.9) | collective-permute-done | bytes 1052704 | tf_op jit(solution)/shard_map/ppermute | solution.py:210
  72.7 5.0 %collective-permute-start.10 = (bf16[4112,128]{1,0:T(8,128)(2,1)}, bf16[4112,128]{1,0:T(8,128)(2,1)S(1)}, u32[]{:S(2)}, u32[]{:S(2)}) collective-permute-start(bf16[4112,128]{1,0:T(8,128)(2,1)} %collective-permute-done.9.refs_1_.t2), channel_id=1, source_target_pairs={{0,16},{1,17},{2,18},{3,19},{4,20},{5,21},{6,22},{7,23},{8,24},{9,... | collective-permute-start | bytes 3158024 | tf_op jit(solution)/shard_map/ppermute | solution.py:210
  77.7 1.3 %collective-permute-start.12 = (bf16[4112,128]{1,0:T(8,128)(2,1)}, bf16[4112,128]{1,0:T(8,128)(2,1)S(1)}, u32[]{:S(2)}, u32[]{:S(2)}) collective-permute-start(bf16[4112,128]{1,0:T(8,128)(2,1)} %collective-permute-done.11.b3r), channel_id=1, source_target_pairs={{0,256},{1,257},{2,258},{3,259},{4,260},{5,261},{6,262},{7,263},{8... | collective-permute-start | bytes 3158024 | tf_op jit(solution)/shard_map/ppermute | solution.py:210
  79.0 1.2 %copy-done.2 = bf16[4112,128]{1,0:T(8,128)(2,1)S(1)} copy-done((bf16[4112,128]{1,0:T(8,128)(2,1)S(1)}, bf16[4112,128]{1,0:T(8,128)(2,1)}, u32[]{:S(2)}) %copy-start.2) | copy-done | bytes 1052696
  80.3 8.5 %shard_map.28.refs_0_ = f32[16,128,128]{2,1,0:T(8,128)S(1)} custom-call(s32[128]{0:T(128)S(1)} %get-tuple-element.12.own_table, s32[32]{0:T(128)S(1)} %bitcast_select_fusion.cells, s32[6]{0:T(128)S(1)} %stack.31.meta, bf16[4096,128]{1,0:T(8,128)(2,1)S(1)} %bitcast.21, bf16[4112,128]{1,0:T(8,128)(2,1)S(1)} %pad_maximum_fusion.1.refs_0_.t0, ...), custom_call_target="tpu_custom_call" | custom-call | flops 23000000512 | tf_op jit(solution)/shard_map/pallas_call | solution.py:185
  88.8 3.4 %shard_map.29.before = f32[16,128,128]{2,1,0:T(8,128)S(1)} custom-call(s32[128]{0:T(128)S(1)} %get-tuple-element.12.own_table, s32[32]{0:T(128)S(1)} %bitcast_select_fusion.cells, s32[6]{0:T(128)S(1)} %stack.31.meta, bf16[4096,128]{1,0:T(8,128)(2,1)S(1)} %bitcast.22, f32[16,128,128]{2,1,0:T(8,128)S(1)} %shard_map.28.refs_0_, ...), custom_call_target="tpu_custom_call" | custom-call | flops 5750000128 | tf_op jit(solution)/shard_map/pallas_call | solution.py:185
  92.2 1.3 %collective-permute-done.12.b3s = bf16[4112,128]{1,0:T(8,128)(2,1)S(1)} collective-permute-done((bf16[4112,128]{1,0:T(8,128)(2,1)}, bf16[4112,128]{1,0:T(8,128)(2,1)S(1)}, u32[]{:S(2)}, u32[]{:S(2)}) %collective-permute-start.12) | collective-permute-done | bytes 1052704 | tf_op jit(solution)/shard_map/ppermute | solution.py:210
  93.5 9.5 %shard_map.30 = f32[16,128,128]{2,1,0:T(8,128)} custom-call(s32[128]{0:T(128)S(1)} %get-tuple-element.12.own_table, s32[32]{0:T(128)S(1)} %bitcast_select_fusion.cells, s32[6]{0:T(128)S(1)} %stack.31.meta, bf16[4096,128]{1,0:T(8,128)(2,1)S(1)} %bitcast.23, f32[16,128,128]{2,1,0:T(8,128)S(1)} %shard_map.29.before, ...), custom_call_target="tpu_custom_call" | custom-call | flops 11500000256 | tf_op jit(solution)/shard_map/pallas_call | solution.py:185
  (22 shorter events, 0.3 us)
Async XLA Ops:
  0.0 6.5 %copy-start = (bf16[1,1,32,128,128]{4,3,2,1,0:T(8,128)(2,1)S(1)}, bf16[1,1,32,128,128]{4,3,2,1,0:T(8,128)(2,1)}, u32[]{:S(2)}) copy-start(bf16[1,1,32,128,128]{4,3,2,1,0:T(8,128)(2,1)} %param.2) | copy-start | bytes 3145732
  0.0 6.1 %copy-start.3 = (s32[1,1,2,32]{3,2,1,0:T(2,128)S(1)}, s32[1,1,2,32]{3,2,1,0:T(2,128)}, u32[]{:S(2)}) copy-start(s32[1,1,2,32]{3,2,1,0:T(2,128)} %param.3) | copy-start | bytes 772
  1.2 11.5 %collective-permute-start = (bf16[2064,128]{1,0:T(8,128)(2,1)S(1)}, bf16[2064,128]{1,0:T(8,128)(2,1)}, u32[]{:S(2)}, u32[]{:S(2)}) collective-permute-start(bf16[2064,128]{1,0:T(8,128)(2,1)S(1)} %slice.25), channel_id=1, source_target_pairs={{0,64},{13,77},{14,78},{15,79},{16,80},{17,81},{30,94},{31,95},{32... | collective-permute-start | bytes 1585160 | tf_op jit(solution)/shard_map/ppermute | solution.py:210
  7.5 17.9 %collective-permute-start.5 = (bf16[4112,128]{1,0:T(8,128)(2,1)}, bf16[4112,128]{1,0:T(8,128)(2,1)S(1)}, u32[]{:S(2)}, u32[]{:S(2)}) collective-permute-start(bf16[4112,128]{1,0:T(8,128)(2,1)} %pad_maximum_fusion), channel_id=1, source_target_pairs={{0,15},{1,0},{2,1},{3,2},{4,3},{5,4},{6,5},{7,6},{8,7},{9,8},{10,9... | collective-permute-start | bytes 3158024 | tf_op jit(solution)/shard_map/ppermute | solution.py:210
  9.3 10.2 %collective-permute-start.2 = (bf16[2064,128]{1,0:T(8,128)(2,1)S(1)}, bf16[2064,128]{1,0:T(8,128)(2,1)}, u32[]{:S(2)}, u32[]{:S(2)}) collective-permute-start(bf16[2064,128]{1,0:T(8,128)(2,1)S(1)} %slice.26), channel_id=1, source_target_pairs={{0,192},{13,205},{14,206},{15,207},{16,208},{17,209},{30,222},{31,... | collective-permute-start | bytes 1585160 | tf_op jit(solution)/shard_map/ppermute | solution.py:210
  13.5 14.8 %collective-permute-start.1 = (bf16[2064,128]{1,0:T(8,128)(2,1)}, bf16[2064,128]{1,0:T(8,128)(2,1)}, u32[]{:S(2)}, u32[]{:S(2)}) collective-permute-start(bf16[2064,128]{1,0:T(8,128)(2,1)} %broadcast_select_fusion.1), channel_id=1, source_target_pairs={{0,64},{9,73},{10,74},{11,75},{12,76},{13,77},{14,78},{15,79},{16,... | collective-permute-start | bytes 1585160 | tf_op jit(solution)/shard_map/ppermute | solution.py:210
  20.4 14.8 %collective-permute-start.3 = (bf16[2064,128]{1,0:T(8,128)(2,1)}, bf16[2064,128]{1,0:T(8,128)(2,1)}, u32[]{:S(2)}, u32[]{:S(2)}) collective-permute-start(bf16[2064,128]{1,0:T(8,128)(2,1)} %broadcast_select_fusion), channel_id=1, source_target_pairs={{0,192},{1,193},{2,194},{3,195},{4,196},{13,205},{14,206},{15,207}... | collective-permute-start | bytes 1585160 | tf_op jit(solution)/shard_map/ppermute | solution.py:210
  25.4 29.6 %collective-permute-start.7 = (bf16[4112,128]{1,0:T(8,128)(2,1)S(1)}, bf16[4112,128]{1,0:T(8,128)(2,1)}, u32[]{:S(2)}, u32[]{:S(2)}) collective-permute-start(bf16[4112,128]{1,0:T(8,128)(2,1)S(1)} %collective-permute-done.5.refs_2_.b1r), channel_id=1, source_target_pairs={{0,15},{1,0},{2,1},{3,2},{4,3},{5,4},{6,5},{7,6},{8,7},{9,8},{10,9... | collective-permute-start | bytes 3158024 | tf_op jit(solution)/shard_map/ppermute | solution.py:210
  27.1 31.4 %collective-permute-start.6 = (bf16[4112,128]{1,0:T(8,128)(2,1)S(1)}, bf16[4112,128]{1,0:T(8,128)(2,1)S(1)}, u32[]{:S(2)}, u32[]{:S(2)}) collective-permute-start(bf16[4112,128]{1,0:T(8,128)(2,1)S(1)} %collective-permute-done.5.refs_2_.b1r), channel_id=1, source_target_pairs={{0,256},{1,257},{2,258},{3,259},{4,260},{5,261},{6,262},{7,263},{8... | collective-permute-start | bytes 3158024 | tf_op jit(solution)/shard_map/ppermute | solution.py:210
  37.9 34.9 %collective-permute-start.9 = (bf16[4112,128]{1,0:T(8,128)(2,1)S(1)}, bf16[4112,128]{1,0:T(8,128)(2,1)}, u32[]{:S(2)}, u32[]{:S(2)}) collective-permute-start(bf16[4112,128]{1,0:T(8,128)(2,1)S(1)} %pad_maximum_fusion.1.refs_0_.t0), channel_id=1, source_target_pairs={{0,288},{1,289},{2,290},{3,291},{4,292},{5,293},{6,294},{7,295},{8... | collective-permute-start | bytes 3158024 | tf_op jit(solution)/shard_map/ppermute | solution.py:210
  51.5 21.2 %collective-permute-start.4 = (bf16[4112,128]{1,0:T(8,128)(2,1)S(1)}, bf16[4112,128]{1,0:T(8,128)(2,1)}, u32[]{:S(2)}, u32[]{:S(2)}) collective-permute-start(bf16[4112,128]{1,0:T(8,128)(2,1)S(1)} %pad_maximum_fusion.1.refs_0_.t0), channel_id=1, source_target_pairs={{0,16},{1,17},{2,18},{3,19},{4,20},{5,21},{6,22},{7,23},{8,24},{9,... | collective-permute-start | bytes 3158024 | tf_op jit(solution)/shard_map/ppermute | solution.py:210
  58.5 1.0 copy-start.1
  59.5 18.2 %collective-permute-start.8 = (bf16[4112,128]{1,0:T(8,128)(2,1)}, bf16[4112,128]{1,0:T(8,128)(2,1)}, u32[]{:S(2)}, u32[]{:S(2)}) collective-permute-start(bf16[4112,128]{1,0:T(8,128)(2,1)} %collective-permute-done.7.refs_4_.b2r), channel_id=1, source_target_pairs={{0,256},{1,257},{2,258},{3,259},{4,260},{5,261},{6,262},{7,263},{8... | collective-permute-start | bytes 3158024 | tf_op jit(solution)/shard_map/ppermute | solution.py:210
  60.8 17.0 %collective-permute-start.11 = (bf16[4112,128]{1,0:T(8,128)(2,1)}, bf16[4112,128]{1,0:T(8,128)(2,1)}, u32[]{:S(2)}, u32[]{:S(2)}) collective-permute-start(bf16[4112,128]{1,0:T(8,128)(2,1)} %collective-permute-done.7.refs_4_.b2r), channel_id=1, source_target_pairs={{0,15},{1,0},{2,1},{3,2},{4,3},{5,4},{6,5},{7,6},{8,7},{9,8},{10,9... | collective-permute-start | bytes 3158024 | tf_op jit(solution)/shard_map/ppermute | solution.py:210
  72.7 19.5 %collective-permute-start.10 = (bf16[4112,128]{1,0:T(8,128)(2,1)}, bf16[4112,128]{1,0:T(8,128)(2,1)S(1)}, u32[]{:S(2)}, u32[]{:S(2)}) collective-permute-start(bf16[4112,128]{1,0:T(8,128)(2,1)} %collective-permute-done.9.refs_1_.t2), channel_id=1, source_target_pairs={{0,16},{1,17},{2,18},{3,19},{4,20},{5,21},{6,22},{7,23},{8,24},{9,... | collective-permute-start | bytes 3158024 | tf_op jit(solution)/shard_map/ppermute | solution.py:210
  77.7 15.8 %collective-permute-start.12 = (bf16[4112,128]{1,0:T(8,128)(2,1)}, bf16[4112,128]{1,0:T(8,128)(2,1)S(1)}, u32[]{:S(2)}, u32[]{:S(2)}) collective-permute-start(bf16[4112,128]{1,0:T(8,128)(2,1)} %collective-permute-done.11.b3r), channel_id=1, source_target_pairs={{0,256},{1,257},{2,258},{3,259},{4,260},{5,261},{6,262},{7,263},{8... | collective-permute-start | bytes 3158024 | tf_op jit(solution)/shard_map/ppermute | solution.py:210
  79.0 1.2 %copy-start.2 = (bf16[4112,128]{1,0:T(8,128)(2,1)S(1)}, bf16[4112,128]{1,0:T(8,128)(2,1)}, u32[]{:S(2)}) copy-start(bf16[4112,128]{1,0:T(8,128)(2,1)} %copy-done.1) | copy-start | bytes 3158020

commit v3 on v2

v3 whole, which is shorter than its diff:
```python
import functools

import jax
import jax.numpy as jnp
from jax import lax
from jax.experimental import pallas as pl
from jax.experimental.pallas import tpu as pltpu
from jax.sharding import PartitionSpec as P

H = 8
STEPS = 4
W = 128
HEAD = 16
TILE = 32 * W
HALF = TILE // 2
LONG = HALF + HEAD
PACK = TILE + HEAD
DENSE = H * W
AXES = ("layer", "row", "col")
BF = jnp.bfloat16


def pairs_of(mesh_shape, target):
    layers, rows, cols = mesh_shape
    flat = lambda at: (at[0] * rows + at[1]) * cols + at[2]
    found = []
    for l in range(layers):
        for r in range(rows):
            for c in range(cols):
                to = target(l, r, c)
                if to is not None:
                    found.append((flat((l, r, c)), flat(to)))
    return found


def is_relay(l, r):
    return r % 2 == l


def from_root(r, c):
    return ((r - c) // 4) % 4


def cells_and_table(coords):
    slots = coords.shape[1]
    values = jnp.arange(W, dtype=jnp.int32)
    used = jnp.any(coords[:, :, None] == values[None, None, :], axis=1)
    below = used[:, None, :] & (values[None, None, :] < coords[:, :, None])
    rank = jnp.sum(below.astype(jnp.int32), axis=2)
    cells = jnp.where(coords[0] >= 0, rank[0] * H + rank[1], H * H)
    hits = cells[None, :] == values[:, None]
    order = jnp.arange(slots, dtype=jnp.int32) - slots
    table = slots + jnp.sum(jnp.where(hits, order[None, :], 0), axis=1)
    return cells, table


def add_product(a_ref, b_ref, a_row, b_row, table_s, cells, base, out):
    def block_of(ref, at, cell):
        return ref[pl.ds(pl.multiple_of(table_s[at, cell] * W, W), W), :]

    @pl.loop(0, 16, unroll=4)
    def _(q):
        cell = cells[base + q]
        held = jnp.minimum(cell, H * H - 1)
        r, c = held // H, held % H
        left = jnp.concatenate([block_of(a_ref, a_row, r * H + k) for k in range(H)], axis=1)
        right = jnp.concatenate([block_of(b_ref, b_row, k * H + c) for k in range(H)], axis=0)
        block = jnp.dot(left, right, preferred_element_type=jnp.float32)
        out[q] += jnp.where(cell < H * H, block, jnp.zeros_like(block))


def product_kernel(jobs, lefts, last_step, has_before, own_table, cells, meta, own, *refs):
    before, refs = (refs[0], refs[1:]) if has_before else (None, refs)
    tiles, refs = refs[:lefts], refs[lefts:]
    rights, refs = refs[:2 * last_step], refs[2 * last_step:]
    out, a_all, b_all, heads, table_v, table_s, sems = refs
    relay = meta[0] == 1
    spread = meta[0] == 0
    steps = [meta[1 + i] for i in range(4)]
    plans = [job(steps) for job in jobs]
    actives = []
    for j, (choices, step) in enumerate(plans):
        active = choices[0][0]
        for holds, _ in choices[1:]:
            active = jnp.logical_or(active, holds)
        actives.append(active)

        def start(src, at, row, holds):
            @pl.when(holds)
            def _():
                pltpu.make_async_copy(src.at[pl.ds(0, TILE)], at.at[j, pl.ds(0, TILE)], sems.at[row]).start()
                pltpu.make_async_copy(src.at[pl.ds(TILE, HEAD)], heads.at[row], sems.at[2 * len(plans) + row]).start()

        for holds, i in choices:
            start(tiles[i], a_all, 2 * j, holds)

        if isinstance(step, int):
            start(rights[2 * step - 2], b_all, 2 * j + 1, jnp.logical_and(active, relay))
            start(rights[2 * step - 1], b_all, 2 * j + 1, jnp.logical_and(active, spread))
            continue

        @pl.when(jnp.logical_and(active, step == 0))
        def _():
            pltpu.make_async_copy(own, b_all.at[j, pl.ds(0, TILE)], sems.at[2 * j + 1]).start()
            pltpu.make_async_copy(tiles[0].at[pl.ds(TILE, HEAD)], heads.at[2 * j + 1], sems.at[2 * len(plans) + 2 * j + 1]).start()

        for s in range(1, last_step + 1):
            holds = jnp.logical_and(active, step == s)
            start(rights[2 * s - 2], b_all, 2 * j + 1, jnp.logical_and(holds, relay))
            start(rights[2 * s - 1], b_all, 2 * j + 1, jnp.logical_and(holds, spread))

    def wait(row, at):
        pltpu.make_async_copy(own, at.at[row // 2, pl.ds(0, TILE)], sems.at[row]).wait()

    for j in range(len(plans)):
        a_all[j, TILE:, :] = jnp.zeros((W, W), BF)
        b_all[j, TILE:, :] = jnp.zeros((W, W), BF)
    out[...] = jnp.zeros_like(out) if before is None else before[...]
    table_v[...] = jnp.zeros_like(table_v)
    for j, active in enumerate(actives):
        @pl.when(active)
        def _():
            for row in (2 * j, 2 * j + 1):
                pltpu.make_async_copy(own.at[pl.ds(0, HEAD)], heads.at[row], sems.at[2 * len(plans) + row]).wait()
                table_v[row:row + 1, :] = heads[row, 0:1, :].astype(jnp.float32).astype(jnp.int32)
    copy = pltpu.make_async_copy(table_v, table_s, sems.at[4 * len(plans)])
    copy.start()
    copy.wait()
    for j, ((_, step), active) in enumerate(zip(plans, actives)):
        if not isinstance(step, int):
            @pl.when(jnp.logical_and(active, step == 0))
            def _():
                @pl.loop(0, H * H)
                def _(i):
                    table_s[2 * j + 1, i] = own_table[i]

        @pl.when(active)
        def _():
            wait(2 * j, a_all)
            wait(2 * j + 1, b_all)
            add_product(a_all.at[j], b_all.at[j], 2 * j, 2 * j + 1, table_s, cells, meta[5], out)


def pick_kernel(meta, *refs):
    lows, highs, out, sems = refs[:4], refs[4:8], refs[8], refs[9]
    for away in range(4):
        @pl.when(meta[6] == away)
        def _():
            one = pltpu.make_async_copy(lows[away].at[pl.ds(0, HALF)], out.at[pl.ds(0, HALF)], sems.at[0])
            two = pltpu.make_async_copy(highs[away], out.at[pl.ds(HALF, LONG)], sems.at[1])
            one.start()
            two.start()
            one.wait()
            two.wait()


def pack_kernel(tile, head, out, sems):
    one = pltpu.make_async_copy(tile, out.at[pl.ds(0, TILE)], sems.at[0])
    two = pltpu.make_async_copy(head, out.at[pl.ds(TILE, HEAD)], sems.at[1])
    one.start()
    two.start()
    one.wait()
    two.wait()


SMEM = pl.BlockSpec(memory_space=pltpu.SMEM)
VMEM = pl.BlockSpec(memory_space=pltpu.VMEM)
ANY = pl.BlockSpec(memory_space=pl.ANY)


def cost(us):
    return pl.CostEstimate(flops=int(us * 1.15e9), bytes_accessed=0, transcendentals=0)


def same_kernel(ref, out):
    del ref, out


def held(value, us):
    return pl.pallas_call(
        same_kernel,
        out_shape=jax.ShapeDtypeStruct(value.shape, value.dtype),
        in_specs=[ANY],
        out_specs=ANY,
        input_output_aliases={0: 0},
        cost_estimate=cost(us),
    )(value)


def pack(tile, head):
    return pl.pallas_call(
        pack_kernel,
        out_shape=jax.ShapeDtypeStruct((PACK, W), BF),
        in_specs=[ANY] * 2,
        out_specs=VMEM,
        scratch_shapes=[pltpu.SemaphoreType.DMA((2,))],
        compiler_params=pltpu.CompilerParams(vmem_limit_bytes=4 * 1024 * 1024),
        cost_estimate=cost(0.1),
    )(tile, head)


def pick(meta, lows, highs):
    return pl.pallas_call(
        pick_kernel,
        out_shape=jax.ShapeDtypeStruct((PACK, W), BF),
        in_specs=[SMEM] + [ANY] * 8,
        out_specs=VMEM,
        scratch_shapes=[pltpu.SemaphoreType.DMA((2,))],
        compiler_params=pltpu.CompilerParams(vmem_limit_bytes=4 * 1024 * 1024),
        cost_estimate=cost(10),
    )(meta, *lows, *highs)


def products(jobs, us, small, tile, before, tiles, rights):
    n = len(jobs)
    kernel = functools.partial(product_kernel, jobs, len(tiles), len(rights) // 2, len(before))
    return pl.pallas_call(
        kernel,
        out_shape=jax.ShapeDtypeStruct((16, W, W), jnp.float32),
        in_specs=[SMEM] * len(small) + [ANY] + [VMEM] * len(before) + [ANY] * (len(tiles) + len(rights)),
        out_specs=VMEM,
        scratch_shapes=[
            pltpu.VMEM((n, TILE + W, W), BF),
            pltpu.VMEM((n, TILE + W, W), BF),
            pltpu.VMEM((2 * n, HEAD, W), BF),
            pltpu.VMEM((8, W), jnp.int32),
            pltpu.SMEM((8, W), jnp.int32),
            pltpu.SemaphoreType.DMA((4 * n + 1,)),
        ],
        compiler_params=pltpu.CompilerParams(vmem_limit_bytes=16 * 1024 * 1024),
        cost_estimate=cost(0.1),
    )(*small, tile, *before, *tiles, *rights)


def body(mesh_shape, x_blocks, x_coords):
    tile = x_blocks.reshape(TILE, W)
    coords = x_coords[0, 0]
    rows, cols = mesh_shape[1:]
    layer, row, col = (lax.axis_index(a) for a in AXES)

    def send(value, target):
        return lax.ppermute(value, AXES, pairs_of(mesh_shape, target))

    def after(value, *others):
        return lax.optimization_barrier((value, *others))[0]

    cells, table = cells_and_table(coords)
    head = jnp.broadcast_to(table.astype(BF)[None, :], (HEAD, W))
    low = after(tile[:LONG])
    high = after(jnp.concatenate([tile[HALF:], head]))
    full = pack(after(tile, low, high), head)

    down = lambda l, r, c: (l, r, (c - 1) % cols) if is_relay(l, r) else None
    over = lambda l, r, c: (1 - l, r, c) if is_relay(l, r) else None
    twin = lambda l, r, c: (l, r ^ 1, c)
    cross = lambda l, r, c: (1 - l, r ^ 2, c)

    def y_hop(starts, by):
        return lambda l, r, c: (l, (r + 4 * by) % rows, c) if from_root(r, c) in starts else None

    steps = [((row ^ bit) - col) % 4 for bit in (0, 1, 2, 3)]
    meta = jnp.stack([(row % 2 == layer).astype(jnp.int32)] + steps + [16 * layer, from_root(row, col)]).astype(jnp.int32)
    small = (table, cells, meta)

    low_up = send(low, y_hop((0,), 1))
    high_dn = send(high, y_hop((0,), -1))
    z1 = send(full, down)
    high_up = send(after(high, low_up), y_hop((0,), 1))
    low_dn = send(after(low, high_dn), y_hop((0,), -1))
    z2 = send(z1, down)
    x1 = send(z1, over)
    low_far = send(low_up, y_hop((1,), 1))
    high_far = send(high_dn, y_hop((3,), -1))
    z3 = send(z2, down)
    x2 = send(after(z2, x1), over)
    t0 = pick(meta, (low, low_up, after(low_far), low_dn), (high, high_up, high_far, high_dn))
    t2 = held(send(t0, cross), 5)
    t1 = send(t0, twin)
    x3 = send(z3, over)
    first = products([lambda s: ([(s[0] < 2, 0)], s[0]), lambda s: ([(s[1] < 2, 1)], s[1])], 0.1, small, tile, (), (t0, after(t1, z3, x2)), (z1, x1))
    t3 = send(after(t2, first), twin)
    second = products([lambda s: ([(s[0] == 2, 0), (s[1] == 2, 1)], 2), lambda s: ([(s[2] < 3, 2)], s[2])], 8, small, tile, (first,), (t0, t1, t2), (z1, x1, z2, x2))
    third = products([lambda s: ([(s[i] == 3, i) for i in range(3)], 3)], 5, small, tile, (second,), (t0, t1, t2), (z1, x1, z2, x2, z3, x3))
    out = products([lambda s: ([(s[3] >= 0, 0)], s[3])], 5, small, tile, (third,), (t3,), (z1, x1, z2, x2, z3, x3))
    return out[None, None]


def solution(mesh):
    return jax.shard_map(
        functools.partial(body, tuple(mesh.shape[a] for a in AXES)),
        mesh=mesh,
        in_specs=(P("col", "row", None, None, None), P("col", "row", None, None)),
        out_specs=P("col", "row", "layer", None, None),
        check_vma=False,
    )
```

time: 105 us -> 99.6 us (0.949); the launches traced: 103 us -> 99.1 us
  starting transfers between devices: 48.8 us -> 57.2 us
  other arithmetic: 5.82 us -> 1.22 us
  waiting for transfers between devices: 22.3 us -> 18.3 us
  local copies, waits for them, and re-layouts: 4.58 us -> 2.09 us
  Pallas kernels: 21.4 us -> 20.1 us
    ppermute x13 -> x15, starting transfers between devices: 48.8 us -> 57.2 us  [send(): return lax.ppermute(value, AXES, pairs_of(mesh_shape, target))]
    select_n x4 -> x0, other arithmetic: 4.32 us -> none  [the longest x1 1.46 us: body(): jnp.where(away == 0, low, jnp.where(away == 1, up1, jnp.where(away == 2,...]
    ppermute x13 -> x15, waiting for transfers between devices: 22.3 us -> 18.3 us  [send(): return lax.ppermute(value, AXES, pairs_of(mesh_shape, target))]
    unnamed x8 -> x4, local copies, waits for them, and re-layouts: 2.24 us -> 0.01 us
    pallas_call x3 -> x7, Pallas kernels: 21.4 us -> 20.1 us  [the longest x4 17.2 us: products(): pl.pallas_call(kernel, out_shape=jax.ShapeDtypeStruct((16, W, W), jnp.flo...]
  transfers between devices with their start and end apart: 13 -> 15, of which waited for: 5 -> 4; matrix products, arithmetic and copies ran while one was open for 7% -> 1% of each run, Pallas kernels for 12% -> 15%
where the time goes in v3:
time: 99.6 us; the launch traced here: 99.1 us
  starting transfers between devices  57.2 us (57%)
  Pallas kernels  20.1 us (20%)
  waiting for transfers between devices  18.3 us (18%)
  local copies, waits for them, and re-layouts  2.09 us (2%)
  other arithmetic  1.22 us (1%)
    ppermute x15, starting transfers between devices, send(): return lax.ppermute(value, AXES, pairs_of(mesh_shape, target))  57.2 us
    ppermute x15, waiting for transfers between devices, send(): return lax.ppermute(value, AXES, pairs_of(mesh_shape, target))  18.3 us
    pallas_call x4, Pallas kernels, products(): pl.pallas_call(kernel, out_shape=jax.ShapeDtypeStruct((16, W, W), jnp.flo...  17.2 us
    pallas_call x1, Pallas kernels, pick(): pl.pallas_call(pick_kernel, out_shape=jax.ShapeDtypeStruct((PACK, W), BF)...  2.78 us
  transfers between devices with their start and end apart: 15, of which 4 were waited for; matrix products, arithmetic and copies ran while one was open for 1% of the time, Pallas kernels for 15%

profile of v3, /device:TPU:1, one launch (start us, length us, event | category | flops | bytes accessed | tf_op | source)
XLA Modules:
  0.0 99.1 jit_solution(16320131248399306365)
XLA Ops:
  0.0 2.0 %slice.25.refs_0_ = bf16[2064,128]{1,0:T(8,128)(2,1)} slice(bf16[4096,128]{1,0:T(8,128)(2,1)} %bitcast.21), slice={[0:2064], [0:128]} | slice | bytes 1056768 | tf_op jit(solution)/shard_map/slice | solution.py:249
  2.0 4.8 %collective-permute-start = (bf16[2064,128]{1,0:T(8,128)(2,1)}, bf16[2064,128]{1,0:T(8,128)(2,1)}, u32[]{:S(2)}, u32[]{:S(2)}) collective-permute-start(bf16[2064,128]{1,0:T(8,128)(2,1)} %slice.25.refs_0_), channel_id=1, source_target_pairs={{0,64},{13,77},{14,78},{15,79},{16,80},{17,81},{30,94},{31,95},{32... | collective-permute-start | bytes 1585160 | tf_op jit(solution)/shard_map/ppermute | solution.py:242
  6.8 0.1 fusion
  6.9 0.2 convert_reduce_fusion
  7.1 0.1 select_reduce_fusion
  7.3 0.8 pad_maximum_fusion.refs_4_
  8.1 2.9 %collective-permute-start.2 = (bf16[2064,128]{1,0:T(8,128)(2,1)}, bf16[2064,128]{1,0:T(8,128)(2,1)}, u32[]{:S(2)}, u32[]{:S(2)}) collective-permute-start(bf16[2064,128]{1,0:T(8,128)(2,1)} %pad_maximum_fusion.refs_4_), channel_id=1, source_target_pairs={{0,192},{13,205},{14,206},{15,207},{16,208},{17,209},{30,222},{31,... | collective-permute-start | bytes 1585160 | tf_op jit(solution)/shard_map/ppermute | solution.py:242
  11.0 0.1 shard_map.29
  11.1 0.7 collective-permute-start.7
  11.8 1.9 %collective-permute-done.refs_1_ = bf16[2064,128]{1,0:T(8,128)(2,1)} collective-permute-done((bf16[2064,128]{1,0:T(8,128)(2,1)}, bf16[2064,128]{1,0:T(8,128)(2,1)}, u32[]{:S(2)}, u32[]{:S(2)}) %collective-permute-start) | collective-permute-done | bytes 528416 | tf_op jit(solution)/shard_map/ppermute | solution.py:242
  13.7 4.9 %collective-permute-start.4 = (bf16[2064,128]{1,0:T(8,128)(2,1)}, bf16[2064,128]{1,0:T(8,128)(2,1)}, u32[]{:S(2)}, u32[]{:S(2)}) collective-permute-start(bf16[2064,128]{1,0:T(8,128)(2,1)} %pad_maximum_fusion.refs_4_), channel_id=1, source_target_pairs={{0,64},{13,77},{14,78},{15,79},{16,80},{17,81},{30,94},{31,95},{32... | collective-permute-start | bytes 1585160 | tf_op jit(solution)/shard_map/ppermute | solution.py:242
  18.6 1.5 %collective-permute-start.1 = (bf16[2064,128]{1,0:T(8,128)(2,1)}, bf16[2064,128]{1,0:T(8,128)(2,1)}, u32[]{:S(2)}, u32[]{:S(2)}) collective-permute-start(bf16[2064,128]{1,0:T(8,128)(2,1)} %collective-permute-done.refs_1_), channel_id=1, source_target_pairs={{9,73},{10,74},{11,75},{12,76},{26,90},{27,91},{28,92},{29,93},{43... | collective-permute-start | bytes 1585160 | tf_op jit(solution)/shard_map/ppermute | solution.py:242
  20.1 0.0 collective-permute-done.2.refs_7_
  20.1 4.8 %collective-permute-start.3 = (bf16[2064,128]{1,0:T(8,128)(2,1)}, bf16[2064,128]{1,0:T(8,128)(2,1)}, u32[]{:S(2)}, u32[]{:S(2)}) collective-permute-start(bf16[2064,128]{1,0:T(8,128)(2,1)} %slice.25.refs_0_), channel_id=1, source_target_pairs={{0,192},{13,205},{14,206},{15,207},{16,208},{17,209},{30,222},{31,... | collective-permute-start | bytes 1585160 | tf_op jit(solution)/shard_map/ppermute | solution.py:242
  24.9 1.5 %collective-permute-start.5 = (bf16[2064,128]{1,0:T(8,128)(2,1)}, bf16[2064,128]{1,0:T(8,128)(2,1)}, u32[]{:S(2)}, u32[]{:S(2)}) collective-permute-start(bf16[2064,128]{1,0:T(8,128)(2,1)} %collective-permute-done.2.refs_7_), channel_id=1, source_target_pairs={{1,193},{2,194},{3,195},{4,196},{18,210},{19,211},{20,212},{21,213... | collective-permute-start | bytes 1585160 | tf_op jit(solution)/shard_map/ppermute | solution.py:242
  26.3 0.1 stack.35.meta
  26.4 1.3 %collective-permute-start.10 = (bf16[4112,128]{1,0:T(8,128)(2,1)S(1)}, bf16[4112,128]{1,0:T(8,128)(2,1)S(1)}, u32[]{:S(2)}, u32[]{:S(2)}) collective-permute-start(bf16[4112,128]{1,0:T(8,128)(2,1)S(1)} %collective-permute-done.7.refs_2_.refs_4_), channel_id=1, source_target_pairs={{0,256},{1,257},{2,258},{3,259},{4,260},{5,261},{6,262},{7,263},{8... | collective-permute-start | bytes 3158024 | tf_op jit(solution)/shard_map/ppermute | solution.py:242
  27.7 1.6 %collective-permute-start.8 = (bf16[4112,128]{1,0:T(8,128)(2,1)S(1)}, bf16[4112,128]{1,0:T(8,128)(2,1)}, u32[]{:S(2)}, u32[]{:S(2)}) collective-permute-start(bf16[4112,128]{1,0:T(8,128)(2,1)S(1)} %collective-permute-done.7.refs_2_.refs_4_), channel_id=1, source_target_pairs={{0,15},{1,0},{2,1},{3,2},{4,3},{5,4},{6,5},{7,6},{8,7},{9,8},{10,9... | collective-permute-start | bytes 3158024 | tf_op jit(solution)/shard_map/ppermute | solution.py:242
  29.4 2.3 %collective-permute-done.3.refs_3_ = bf16[2064,128]{1,0:T(8,128)(2,1)} collective-permute-done((bf16[2064,128]{1,0:T(8,128)(2,1)}, bf16[2064,128]{1,0:T(8,128)(2,1)}, u32[]{:S(2)}, u32[]{:S(2)}) %collective-permute-start.3) | collective-permute-done | bytes 528416 | tf_op jit(solution)/shard_map/ppermute | solution.py:242
  31.6 2.8 %shard_map.28.refs_0_.refs_1_ = bf16[4112,128]{1,0:T(8,128)(2,1)} custom-call(s32[7]{0:T(128)S(1)} %stack.35.meta, bf16[2064,128]{1,0:T(8,128)(2,1)} %slice.25.refs_0_, bf16[2064,128]{1,0:T(8,128)(2,1)} %collective-permute-done.refs_1_, bf16[2064,128]{1,0:T(8,128)(2,1)} %collective-permute-done.1.refs_2_, bf16[2064,128]{1,0:T(8,128)(2,1)} %collective-permute-done.3.refs_3_, ...), custom_call_target="tpu_custom_call" | custom-call | flops 11500000256 | tf_op jit(solution)/shard_map/pallas_call | solution.py:203
  34.4 11.7 %collective-permute-start.12 = (bf16[4112,128]{1,0:T(8,128)(2,1)}, bf16[4112,128]{1,0:T(8,128)(2,1)}, u32[]{:S(2)}, u32[]{:S(2)}) collective-permute-start(bf16[4112,128]{1,0:T(8,128)(2,1)} %shard_map.28.refs_0_.refs_1_), channel_id=1, source_target_pairs={{0,288},{1,289},{2,290},{3,291},{4,292},{5,293},{6,294},{7,295},{8... | collective-permute-start | bytes 3158024 | tf_op jit(solution)/shard_map/ppermute | solution.py:242
  46.2 6.1 %collective-permute-start.6 = (bf16[4112,128]{1,0:T(8,128)(2,1)}, bf16[4112,128]{1,0:T(8,128)(2,1)}, u32[]{:S(2)}, u32[]{:S(2)}) collective-permute-start(bf16[4112,128]{1,0:T(8,128)(2,1)} %shard_map.28.refs_0_.refs_1_), channel_id=1, source_target_pairs={{0,16},{1,17},{2,18},{3,19},{4,20},{5,21},{6,22},{7,23},{8,24},{9,... | collective-permute-start | bytes 3158024 | tf_op jit(solution)/shard_map/ppermute | solution.py:242
  52.3 1.3 %collective-permute-start.11 = (bf16[4112,128]{1,0:T(8,128)(2,1)}, bf16[4112,128]{1,0:T(8,128)(2,1)}, u32[]{:S(2)}, u32[]{:S(2)}) collective-permute-start(bf16[4112,128]{1,0:T(8,128)(2,1)} %collective-permute-done.8.refs_6_.refs_4_), channel_id=1, source_target_pairs={{0,256},{1,257},{2,258},{3,259},{4,260},{5,261},{6,262},{7,263},{8... | collective-permute-start | bytes 3158024 | tf_op jit(solution)/shard_map/ppermute | solution.py:242
  53.6 1.7 %collective-permute-start.9 = (bf16[4112,128]{1,0:T(8,128)(2,1)}, bf16[4112,128]{1,0:T(8,128)(2,1)}, u32[]{:S(2)}, u32[]{:S(2)}) collective-permute-start(bf16[4112,128]{1,0:T(8,128)(2,1)} %collective-permute-done.8.refs_6_.refs_4_), channel_id=1, source_target_pairs={{0,15},{1,0},{2,1},{3,2},{4,3},{5,4},{6,5},{7,6},{8,7},{9,8},{10,9... | collective-permute-start | bytes 3158024 | tf_op jit(solution)/shard_map/ppermute | solution.py:242
  55.2 9.9 %collective-permute-done.12.ref = bf16[4112,128]{1,0:T(8,128)(2,1)} collective-permute-done((bf16[4112,128]{1,0:T(8,128)(2,1)}, bf16[4112,128]{1,0:T(8,128)(2,1)}, u32[]{:S(2)}, u32[]{:S(2)}) %collective-permute-start.12) | collective-permute-done | bytes 1052704 | tf_op jit(solution)/shard_map/ppermute | solution.py:242
  65.1 4.2 %collective-permute-done.11.refs_7_.refs_5_ = bf16[4112,128]{1,0:T(8,128)(2,1)} collective-permute-done((bf16[4112,128]{1,0:T(8,128)(2,1)}, bf16[4112,128]{1,0:T(8,128)(2,1)}, u32[]{:S(2)}, u32[]{:S(2)}) %collective-permute-start.11) | collective-permute-done | bytes 1052704 | tf_op jit(solution)/shard_map/ppermute | solution.py:242
  69.3 1.3 %collective-permute-start.13 = (bf16[4112,128]{1,0:T(8,128)(2,1)}, bf16[4112,128]{1,0:T(8,128)(2,1)S(1)}, u32[]{:S(2)}, u32[]{:S(2)}) collective-permute-start(bf16[4112,128]{1,0:T(8,128)(2,1)} %collective-permute-done.9.refs_8_.refs_6_), channel_id=1, source_target_pairs={{0,256},{1,257},{2,258},{3,259},{4,260},{5,261},{6,262},{7,263},{8... | collective-permute-start | bytes 3158024 | tf_op jit(solution)/shard_map/ppermute | solution.py:242
  70.6 6.7 %shard_map.30.refs_0_ = f32[16,128,128]{2,1,0:T(8,128)S(1)} custom-call(s32[128]{0:T(128)S(1)} %get-tuple-element.18.own_table, s32[32]{0:T(128)S(1)} %bitcast_select_fusion.cells, s32[7]{0:T(128)S(1)} %stack.35.meta, bf16[4096,128]{1,0:T(8,128)(2,1)S(1)} %bitcast.23, bf16[4112,128]{1,0:T(8,128)(2,1)} %shard_map.28.refs_0_.refs_1_, ...), custom_call_target="tpu_custom_call" | custom-call | flops 115000000 | tf_op jit(solution)/shard_map/pallas_call | solution.py:217
  77.3 11.2 %collective-permute-start.14 = (bf16[4112,128]{1,0:T(8,128)(2,1)}, bf16[4112,128]{1,0:T(8,128)(2,1)S(1)}, u32[]{:S(2)}, u32[]{:S(2)}) collective-permute-start(bf16[4112,128]{1,0:T(8,128)(2,1)} %shard_map.31.refs_3_), channel_id=1, source_target_pairs={{0,16},{1,17},{2,18},{3,19},{4,20},{5,21},{6,22},{7,23},{8,24},{9,... | collective-permute-start | bytes 3158024 | tf_op jit(solution)/shard_map/ppermute | solution.py:242
  88.5 1.4 %shard_map.32.refs_0_ = f32[16,128,128]{2,1,0:T(8,128)S(1)} custom-call(s32[128]{0:T(128)S(1)} %get-tuple-element.18.own_table, s32[32]{0:T(128)S(1)} %bitcast_select_fusion.cells, s32[7]{0:T(128)S(1)} %stack.35.meta, bf16[4096,128]{1,0:T(8,128)(2,1)S(1)} %bitcast.24, f32[16,128,128]{2,1,0:T(8,128)S(1)} %shard_map.30.refs_0_, ...), custom_call_target="tpu_custom_call" | custom-call | flops 115000000 | tf_op jit(solution)/shard_map/pallas_call | solution.py:217
  89.9 4.0 %shard_map.33.refs_0_ = f32[16,128,128]{2,1,0:T(8,128)S(1)} custom-call(s32[128]{0:T(128)S(1)} %get-tuple-element.18.own_table, s32[32]{0:T(128)S(1)} %bitcast_select_fusion.cells, s32[7]{0:T(128)S(1)} %stack.35.meta, bf16[4096,128]{1,0:T(8,128)(2,1)S(1)} %bitcast.25, f32[16,128,128]{2,1,0:T(8,128)S(1)} %shard_map.32.refs_0_, ...), custom_call_target="tpu_custom_call" | custom-call | flops 115000000 | tf_op jit(solution)/shard_map/pallas_call | solution.py:217
  94.0 5.1 %shard_map.34 = f32[16,128,128]{2,1,0:T(8,128)} custom-call(s32[128]{0:T(128)S(1)} %get-tuple-element.18.own_table, s32[32]{0:T(128)S(1)} %bitcast_select_fusion.cells, s32[7]{0:T(128)S(1)} %stack.35.meta, bf16[4096,128]{1,0:T(8,128)(2,1)S(1)} %bitcast.26, f32[16,128,128]{2,1,0:T(8,128)S(1)} %shard_map.33.refs_0_, ...), custom_call_target="tpu_custom_call" | custom-call | flops 115000000 | tf_op jit(solution)/shard_map/pallas_call | solution.py:217
  (21 shorter events, 0.1 us)
Async XLA Ops:
  0.0 6.8 %copy-start = (bf16[1,1,32,128,128]{4,3,2,1,0:T(8,128)(2,1)S(1)}, bf16[1,1,32,128,128]{4,3,2,1,0:T(8,128)(2,1)}, u32[]{:S(2)}) copy-start(bf16[1,1,32,128,128]{4,3,2,1,0:T(8,128)(2,1)} %param.2) | copy-start | bytes 3145732
  0.0 6.8 %copy-start.1 = (s32[1,1,2,32]{3,2,1,0:T(2,128)S(1)}, s32[1,1,2,32]{3,2,1,0:T(2,128)}, u32[]{:S(2)}) copy-start(s32[1,1,2,32]{3,2,1,0:T(2,128)} %param.3) | copy-start | bytes 772
  2.0 11.8 %collective-permute-start = (bf16[2064,128]{1,0:T(8,128)(2,1)}, bf16[2064,128]{1,0:T(8,128)(2,1)}, u32[]{:S(2)}, u32[]{:S(2)}) collective-permute-start(bf16[2064,128]{1,0:T(8,128)(2,1)} %slice.25.refs_0_), channel_id=1, source_target_pairs={{0,64},{13,77},{14,78},{15,79},{16,80},{17,81},{30,94},{31,95},{32... | collective-permute-start | bytes 1585160 | tf_op jit(solution)/shard_map/ppermute | solution.py:242
  8.1 12.0 %collective-permute-start.2 = (bf16[2064,128]{1,0:T(8,128)(2,1)}, bf16[2064,128]{1,0:T(8,128)(2,1)}, u32[]{:S(2)}, u32[]{:S(2)}) collective-permute-start(bf16[2064,128]{1,0:T(8,128)(2,1)} %pad_maximum_fusion.refs_4_), channel_id=1, source_target_pairs={{0,192},{13,205},{14,206},{15,207},{16,208},{17,209},{30,222},{31,... | collective-permute-start | bytes 1585160 | tf_op jit(solution)/shard_map/ppermute | solution.py:242
  11.1 15.3 %collective-permute-start.7 = (bf16[4112,128]{1,0:T(8,128)(2,1)S(1)}, bf16[4112,128]{1,0:T(8,128)(2,1)S(1)}, u32[]{:S(2)}, u32[]{:S(2)}) collective-permute-start(bf16[4112,128]{1,0:T(8,128)(2,1)S(1)} %shard_map.29), channel_id=1, source_target_pairs={{0,15},{1,0},{2,1},{3,2},{4,3},{5,4},{6,5},{7,6},{8,7},{9,8},{10,9... | collective-permute-start | bytes 3158024 | tf_op jit(solution)/shard_map/ppermute | solution.py:242
  13.7 15.6 %collective-permute-start.4 = (bf16[2064,128]{1,0:T(8,128)(2,1)}, bf16[2064,128]{1,0:T(8,128)(2,1)}, u32[]{:S(2)}, u32[]{:S(2)}) collective-permute-start(bf16[2064,128]{1,0:T(8,128)(2,1)} %pad_maximum_fusion.refs_4_), channel_id=1, source_target_pairs={{0,64},{13,77},{14,78},{15,79},{16,80},{17,81},{30,94},{31,95},{32... | collective-permute-start | bytes 1585160 | tf_op jit(solution)/shard_map/ppermute | solution.py:242
  18.6 9.1 %collective-permute-start.1 = (bf16[2064,128]{1,0:T(8,128)(2,1)}, bf16[2064,128]{1,0:T(8,128)(2,1)}, u32[]{:S(2)}, u32[]{:S(2)}) collective-permute-start(bf16[2064,128]{1,0:T(8,128)(2,1)} %collective-permute-done.refs_1_), channel_id=1, source_target_pairs={{9,73},{10,74},{11,75},{12,76},{26,90},{27,91},{28,92},{29,93},{43... | collective-permute-start | bytes 1585160 | tf_op jit(solution)/shard_map/ppermute | solution.py:242
  20.1 11.5 %collective-permute-start.3 = (bf16[2064,128]{1,0:T(8,128)(2,1)}, bf16[2064,128]{1,0:T(8,128)(2,1)}, u32[]{:S(2)}, u32[]{:S(2)}) collective-permute-start(bf16[2064,128]{1,0:T(8,128)(2,1)} %slice.25.refs_0_), channel_id=1, source_target_pairs={{0,192},{13,205},{14,206},{15,207},{16,208},{17,209},{30,222},{31,... | collective-permute-start | bytes 1585160 | tf_op jit(solution)/shard_map/ppermute | solution.py:242
  24.9 6.8 %collective-permute-start.5 = (bf16[2064,128]{1,0:T(8,128)(2,1)}, bf16[2064,128]{1,0:T(8,128)(2,1)}, u32[]{:S(2)}, u32[]{:S(2)}) collective-permute-start(bf16[2064,128]{1,0:T(8,128)(2,1)} %collective-permute-done.2.refs_7_), channel_id=1, source_target_pairs={{1,193},{2,194},{3,195},{4,196},{18,210},{19,211},{20,212},{21,213... | collective-permute-start | bytes 1585160 | tf_op jit(solution)/shard_map/ppermute | solution.py:242
  26.4 25.8 %collective-permute-start.10 = (bf16[4112,128]{1,0:T(8,128)(2,1)S(1)}, bf16[4112,128]{1,0:T(8,128)(2,1)S(1)}, u32[]{:S(2)}, u32[]{:S(2)}) collective-permute-start(bf16[4112,128]{1,0:T(8,128)(2,1)S(1)} %collective-permute-done.7.refs_2_.refs_4_), channel_id=1, source_target_pairs={{0,256},{1,257},{2,258},{3,259},{4,260},{5,261},{6,262},{7,263},{8... | collective-permute-start | bytes 3158024 | tf_op jit(solution)/shard_map/ppermute | solution.py:242
  27.7 24.5 %collective-permute-start.8 = (bf16[4112,128]{1,0:T(8,128)(2,1)S(1)}, bf16[4112,128]{1,0:T(8,128)(2,1)}, u32[]{:S(2)}, u32[]{:S(2)}) collective-permute-start(bf16[4112,128]{1,0:T(8,128)(2,1)S(1)} %collective-permute-done.7.refs_2_.refs_4_), channel_id=1, source_target_pairs={{0,15},{1,0},{2,1},{3,2},{4,3},{5,4},{6,5},{7,6},{8,7},{9,8},{10,9... | collective-permute-start | bytes 3158024 | tf_op jit(solution)/shard_map/ppermute | solution.py:242
  34.4 30.7 %collective-permute-start.12 = (bf16[4112,128]{1,0:T(8,128)(2,1)}, bf16[4112,128]{1,0:T(8,128)(2,1)}, u32[]{:S(2)}, u32[]{:S(2)}) collective-permute-start(bf16[4112,128]{1,0:T(8,128)(2,1)} %shard_map.28.refs_0_.refs_1_), channel_id=1, source_target_pairs={{0,288},{1,289},{2,290},{3,291},{4,292},{5,293},{6,294},{7,295},{8... | collective-permute-start | bytes 3158024 | tf_op jit(solution)/shard_map/ppermute | solution.py:242
  46.2 19.0 %collective-permute-start.6 = (bf16[4112,128]{1,0:T(8,128)(2,1)}, bf16[4112,128]{1,0:T(8,128)(2,1)}, u32[]{:S(2)}, u32[]{:S(2)}) collective-permute-start(bf16[4112,128]{1,0:T(8,128)(2,1)} %shard_map.28.refs_0_.refs_1_), channel_id=1, source_target_pairs={{0,16},{1,17},{2,18},{3,19},{4,20},{5,21},{6,22},{7,23},{8,24},{9,... | collective-permute-start | bytes 3158024 | tf_op jit(solution)/shard_map/ppermute | solution.py:242
  52.3 17.1 %collective-permute-start.11 = (bf16[4112,128]{1,0:T(8,128)(2,1)}, bf16[4112,128]{1,0:T(8,128)(2,1)}, u32[]{:S(2)}, u32[]{:S(2)}) collective-permute-start(bf16[4112,128]{1,0:T(8,128)(2,1)} %collective-permute-done.8.refs_6_.refs_4_), channel_id=1, source_target_pairs={{0,256},{1,257},{2,258},{3,259},{4,260},{5,261},{6,262},{7,263},{8... | collective-permute-start | bytes 3158024 | tf_op jit(solution)/shard_map/ppermute | solution.py:242
  53.6 15.8 %collective-permute-start.9 = (bf16[4112,128]{1,0:T(8,128)(2,1)}, bf16[4112,128]{1,0:T(8,128)(2,1)}, u32[]{:S(2)}, u32[]{:S(2)}) collective-permute-start(bf16[4112,128]{1,0:T(8,128)(2,1)} %collective-permute-done.8.refs_6_.refs_4_), channel_id=1, source_target_pairs={{0,15},{1,0},{2,1},{3,2},{4,3},{5,4},{6,5},{7,6},{8,7},{9,8},{10,9... | collective-permute-start | bytes 3158024 | tf_op jit(solution)/shard_map/ppermute | solution.py:242
  69.3 20.6 %collective-permute-start.13 = (bf16[4112,128]{1,0:T(8,128)(2,1)}, bf16[4112,128]{1,0:T(8,128)(2,1)S(1)}, u32[]{:S(2)}, u32[]{:S(2)}) collective-permute-start(bf16[4112,128]{1,0:T(8,128)(2,1)} %collective-permute-done.9.refs_8_.refs_6_), channel_id=1, source_target_pairs={{0,256},{1,257},{2,258},{3,259},{4,260},{5,261},{6,262},{7,263},{8... | collective-permute-start | bytes 3158024 | tf_op jit(solution)/shard_map/ppermute | solution.py:242
  77.3 16.6 %collective-permute-start.14 = (bf16[4112,128]{1,0:T(8,128)(2,1)}, bf16[4112,128]{1,0:T(8,128)(2,1)S(1)}, u32[]{:S(2)}, u32[]{:S(2)}) collective-permute-start(bf16[4112,128]{1,0:T(8,128)(2,1)} %shard_map.31.refs_3_), channel_id=1, source_target_pairs={{0,16},{1,17},{2,18},{3,19},{4,20},{5,21},{6,22},{7,23},{8,24},{9,... | collective-permute-start | bytes 3158024 | tf_op jit(solution)/shard_map/ppermute | solution.py:242

commit v4 on v3

--- a/solution.py
+++ b/solution.py
@@ -58,7 +58,7 @@
     def block_of(ref, at, cell):
         return ref[pl.ds(pl.multiple_of(table_s[at, cell] * W, W), W), :]
 
-    @pl.loop(0, 16, unroll=4)
+    @pl.loop(0, 16, unroll=8)
     def _(q):
         cell = cells[base + q]
         held = jnp.minimum(cell, H * H - 1)
@@ -69,11 +69,22 @@
         out[q] += jnp.where(cell < H * H, block, jnp.zeros_like(block))
 
 
-def product_kernel(jobs, lefts, last_step, has_before, own_table, cells, meta, own, *refs):
+CUT = 4
+
+
+def spread_copies(src, dst, rows, sem):
+    part = rows // CUT
+    return [pltpu.make_async_copy(src.at[pl.ds(i * part, part)], dst.at[pl.ds(i * part, part)], sem) for i in range(CUT)]
+
+
+def product_kernel(jobs, lefts, last_step, has_before, stored, own_table, cells, meta, own, *refs):
     before, refs = (refs[0], refs[1:]) if has_before else (None, refs)
     tiles, refs = refs[:lefts], refs[lefts:]
     rights, refs = refs[:2 * last_step], refs[2 * last_step:]
     out, a_all, b_all, heads, table_v, table_s, sems = refs
+    if has_before and stored:
+        for copy in spread_copies(before, out, 16, sems.at[4 * len(jobs) + 1]):
+            copy.start()
     relay = meta[0] == 1
     spread = meta[0] == 0
     steps = [meta[1 + i] for i in range(4)]
@@ -88,7 +99,8 @@
         def start(src, at, row, holds):
             @pl.when(holds)
             def _():
-                pltpu.make_async_copy(src.at[pl.ds(0, TILE)], at.at[j, pl.ds(0, TILE)], sems.at[row]).start()
+                for copy in spread_copies(src, at.at[j], TILE, sems.at[row]):
+                    copy.start()
                 pltpu.make_async_copy(src.at[pl.ds(TILE, HEAD)], heads.at[row], sems.at[2 * len(plans) + row]).start()
 
         for holds, i in choices:
@@ -101,7 +113,8 @@
 
         @pl.when(jnp.logical_and(active, step == 0))
         def _():
-            pltpu.make_async_copy(own, b_all.at[j, pl.ds(0, TILE)], sems.at[2 * j + 1]).start()
+            for copy in spread_copies(own, b_all.at[j], TILE, sems.at[2 * j + 1]):
+                copy.start()
             pltpu.make_async_copy(tiles[0].at[pl.ds(TILE, HEAD)], heads.at[2 * j + 1], sems.at[2 * len(plans) + 2 * j + 1]).start()
 
         for s in range(1, last_step + 1):
@@ -115,7 +128,10 @@
     for j in range(len(plans)):
         a_all[j, TILE:, :] = jnp.zeros((W, W), BF)
         b_all[j, TILE:, :] = jnp.zeros((W, W), BF)
-    out[...] = jnp.zeros_like(out) if before is None else before[...]
+    if before is None:
+        out[...] = jnp.zeros_like(out)
+    elif not stored:
+        out[...] = before[...]
     table_v[...] = jnp.zeros_like(table_v)
     for j, active in enumerate(actives):
         @pl.when(active)
@@ -126,6 +142,8 @@
     copy = pltpu.make_async_copy(table_v, table_s, sems.at[4 * len(plans)])
     copy.start()
     copy.wait()
+    if has_before and stored:
+        pltpu.make_async_copy(before, out, sems.at[4 * len(jobs) + 1]).wait()
     for j, ((_, step), active) in enumerate(zip(plans, actives)):
         if not isinstance(step, int):
             @pl.when(jnp.logical_and(active, step == 0))
@@ -146,26 +164,29 @@
     for away in range(4):
         @pl.when(meta[6] == away)
         def _():
-            one = pltpu.make_async_copy(lows[away].at[pl.ds(0, HALF)], out.at[pl.ds(0, HALF)], sems.at[0])
-            two = pltpu.make_async_copy(highs[away], out.at[pl.ds(HALF, LONG)], sems.at[1])
-            one.start()
-            two.start()
-            one.wait()
-            two.wait()
+            copies = spread_copies(lows[away], out, HALF, sems.at[0])
+            copies += spread_copies(highs[away], out.at[pl.ds(HALF, HALF)], HALF, sems.at[1])
+            copies.append(pltpu.make_async_copy(highs[away].at[pl.ds(HALF, HEAD)], out.at[pl.ds(TILE, HEAD)], sems.at[2]))
+            for copy in copies:
+                copy.start()
+    pltpu.make_async_copy(lows[0].at[pl.ds(0, HALF)], out.at[pl.ds(0, HALF)], sems.at[0]).wait()
+    pltpu.make_async_copy(highs[0].at[pl.ds(0, HALF)], out.at[pl.ds(HALF, HALF)], sems.at[1]).wait()
+    pltpu.make_async_copy(highs[0].at[pl.ds(HALF, HEAD)], out.at[pl.ds(TILE, HEAD)], sems.at[2]).wait()
 
 
 def pack_kernel(tile, head, out, sems):
-    one = pltpu.make_async_copy(tile, out.at[pl.ds(0, TILE)], sems.at[0])
-    two = pltpu.make_async_copy(head, out.at[pl.ds(TILE, HEAD)], sems.at[1])
-    one.start()
-    two.start()
-    one.wait()
-    two.wait()
+    copies = spread_copies(tile, out, TILE, sems.at[0])
+    copies.append(pltpu.make_async_copy(head, out.at[pl.ds(TILE, HEAD)], sems.at[1]))
+    for copy in copies:
+        copy.start()
+    pltpu.make_async_copy(tile, out.at[pl.ds(0, TILE)], sems.at[0]).wait()
+    copies[-1].wait()
 
 
 SMEM = pl.BlockSpec(memory_space=pltpu.SMEM)
 VMEM = pl.BlockSpec(memory_space=pltpu.VMEM)
 ANY = pl.BlockSpec(memory_space=pl.ANY)
+HBM = pl.BlockSpec(memory_space=pltpu.HBM)
 
 
 def cost(us):
@@ -193,7 +214,7 @@
         out_shape=jax.ShapeDtypeStruct((PACK, W), BF),
         in_specs=[ANY] * 2,
         out_specs=VMEM,
-        scratch_shapes=[pltpu.SemaphoreType.DMA((2,))],
+        scratch_shapes=[pltpu.SemaphoreType.DMA((3,))],
         compiler_params=pltpu.CompilerParams(vmem_limit_bytes=4 * 1024 * 1024),
         cost_estimate=cost(0.1),
     )(tile, head)
@@ -205,19 +226,20 @@
         out_shape=jax.ShapeDtypeStruct((PACK, W), BF),
         in_specs=[SMEM] + [ANY] * 8,
         out_specs=VMEM,
-        scratch_shapes=[pltpu.SemaphoreType.DMA((2,))],
+        scratch_shapes=[pltpu.SemaphoreType.DMA((3,))],
         compiler_params=pltpu.CompilerParams(vmem_limit_bytes=4 * 1024 * 1024),
         cost_estimate=cost(10),
     )(meta, *lows, *highs)
 
 
-def products(jobs, us, small, tile, before, tiles, rights):
+def products(jobs, us, small, tile, before, tiles, rights, stored=False, far=()):
     n = len(jobs)
-    kernel = functools.partial(product_kernel, jobs, len(tiles), len(rights) // 2, len(before))
+    kernel = functools.partial(product_kernel, jobs, len(tiles), len(rights) // 2, len(before), stored)
     return pl.pallas_call(
         kernel,
         out_shape=jax.ShapeDtypeStruct((16, W, W), jnp.float32),
-        in_specs=[SMEM] * len(small) + [ANY] + [VMEM] * len(before) + [ANY] * (len(tiles) + len(rights)),
+        in_specs=[SMEM] * len(small) + [ANY] + [HBM if stored else VMEM] * len(before)
+        + [HBM if i in far else ANY for i in range(len(tiles))] + [ANY] * len(rights),
         out_specs=VMEM,
         scratch_shapes=[
             pltpu.VMEM((n, TILE + W, W), BF),
@@ -225,7 +247,7 @@
             pltpu.VMEM((2 * n, HEAD, W), BF),
             pltpu.VMEM((8, W), jnp.int32),
             pltpu.SMEM((8, W), jnp.int32),
-            pltpu.SemaphoreType.DMA((4 * n + 1,)),
+            pltpu.SemaphoreType.DMA((4 * n + 2,)),
         ],
         compiler_params=pltpu.CompilerParams(vmem_limit_bytes=16 * 1024 * 1024),
         cost_estimate=cost(0.1),
@@ -248,7 +270,7 @@
     head = jnp.broadcast_to(table.astype(BF)[None, :], (HEAD, W))
     low = after(tile[:LONG])
     high = after(jnp.concatenate([tile[HALF:], head]))
-    full = pack(after(tile, low, high), head)
+    full = pack(tile, head)
 
     down = lambda l, r, c: (l, r, (c - 1) % cols) if is_relay(l, r) else None
     over = lambda l, r, c: (1 - l, r, c) if is_relay(l, r) else None
@@ -263,7 +285,7 @@
     small = (table, cells, meta)
 
     low_up = send(low, y_hop((0,), 1))
-    high_dn = send(high, y_hop((0,), -1))
+    high_dn = send(after(high, full), y_hop((0,), -1))
     z1 = send(full, down)
     high_up = send(after(high, low_up), y_hop((0,), 1))
     low_dn = send(after(low, high_dn), y_hop((0,), -1))
@@ -274,14 +296,14 @@
     z3 = send(z2, down)
     x2 = send(after(z2, x1), over)
     t0 = pick(meta, (low, low_up, after(low_far), low_dn), (high, high_up, high_far, high_dn))
-    t2 = held(send(t0, cross), 5)
     t1 = send(t0, twin)
+    first = products([lambda s: ([(s[0] < 2, 0)], s[0]), lambda s: ([(s[1] < 2, 1)], s[1])], 0.1, small, tile, (), (t0, t1), (z1, x1))
+    t2 = held(after(send(t0, cross), first), 5)
     x3 = send(z3, over)
-    first = products([lambda s: ([(s[0] < 2, 0)], s[0]), lambda s: ([(s[1] < 2, 1)], s[1])], 0.1, small, tile, (), (t0, after(t1, z3, x2)), (z1, x1))
-    t3 = send(after(t2, first), twin)
-    second = products([lambda s: ([(s[0] == 2, 0), (s[1] == 2, 1)], 2), lambda s: ([(s[2] < 3, 2)], s[2])], 8, small, tile, (first,), (t0, t1, t2), (z1, x1, z2, x2))
-    third = products([lambda s: ([(s[i] == 3, i) for i in range(3)], 3)], 5, small, tile, (second,), (t0, t1, t2), (z1, x1, z2, x2, z3, x3))
-    out = products([lambda s: ([(s[3] >= 0, 0)], s[3])], 5, small, tile, (third,), (t3,), (z1, x1, z2, x2, z3, x3))
+    t3 = send(t2, twin)
+    kept0, kept1, kept = (pltpu.with_memory_space_constraint(v, pltpu.HBM) for v in (t0, t1, first))
+    second = products([lambda s: ([(s[0] == 2, 0), (s[1] == 2, 1)], 2), lambda s: ([(s[2] < 3, 2)], s[2]), lambda s: ([(s[3] < 3, 3)], s[3])], 8, small, tile, (kept,), (kept0, kept1, t2, t3), (z1, x1, z2, x2), stored=True, far=(0, 1))
+    out = products([lambda s: ([(s[i] == 3, i) for i in range(4)], 3)], 5, small, tile, (second,), (kept0, kept1, t2, t3), (z1, x1, z2, x2, z3, x3), far=(0, 1))
     return out[None, None]
 
 

time: 99.6 us -> 99.3 us (level)
  waiting for transfers between devices: 18.3 us -> 31.4 us
  starting transfers between devices: 57.2 us -> 46.7 us
  Pallas kernels: 20.1 us -> 16.2 us
    ppermute x15, waiting for transfers between devices: 18.3 us -> 31.4 us  [send(): return lax.ppermute(value, AXES, pairs_of(mesh_shape, target))]
    ppermute x15, starting transfers between devices: 57.2 us -> 46.7 us  [send(): return lax.ppermute(value, AXES, pairs_of(mesh_shape, target))]
    pallas_call x4 -> x3, Pallas kernels: 17.2 us -> 14.2 us  [products(): pl.pallas_call(kernel, out_shape=jax.ShapeDtypeStruct((16, W, W), jnp.flo...]
  transfers between devices with their start and end apart: 15 -> 15, of which waited for: 4 -> 6; matrix products, arithmetic and copies ran while one was open for 1% -> 1% of each run, Pallas kernels for 15% -> 12%
where the time goes in v4:
time: 99.3 us; the launch traced here: 98.9 us
  starting transfers between devices  46.7 us (47%)
  waiting for transfers between devices  31.4 us (32%)
  Pallas kernels  16.2 us (16%)
  local copies, waits for them, and re-layouts  3.07 us (3%)
  other arithmetic  1.24 us (1%)
    ppermute x15, starting transfers between devices, send(): return lax.ppermute(value, AXES, pairs_of(mesh_shape, target))  46.7 us
    ppermute x15, waiting for transfers between devices, send(): return lax.ppermute(value, AXES, pairs_of(mesh_shape, target))  31.4 us
    pallas_call x3, Pallas kernels, products(): pl.pallas_call(kernel, out_shape=jax.ShapeDtypeStruct((16, W, W), jnp.flo...  14.2 us
  transfers between devices with their start and end apart: 15, of which 6 were waited for; matrix products, arithmetic and copies ran while one was open for 1% of the time, Pallas kernels for 12%

profile of v4, /device:TPU:1, one launch (start us, length us, event | category | flops | bytes accessed | tf_op | source)
XLA Modules:
  0.0 98.9 jit_solution(18367745111512085312)
XLA Ops:
  0.0 2.0 %slice.25.refs_0_ = bf16[2064,128]{1,0:T(8,128)(2,1)} slice(bf16[4096,128]{1,0:T(8,128)(2,1)} %bitcast.21), slice={[0:2064], [0:128]} | slice | bytes 1056768 | tf_op jit(solution)/shard_map/slice | solution.py:271
  2.0 4.9 %collective-permute-start = (bf16[2064,128]{1,0:T(8,128)(2,1)}, bf16[2064,128]{1,0:T(8,128)(2,1)}, u32[]{:S(2)}, u32[]{:S(2)}) collective-permute-start(bf16[2064,128]{1,0:T(8,128)(2,1)} %slice.25.refs_0_), channel_id=1, source_target_pairs={{0,64},{13,77},{14,78},{15,79},{16,80},{17,81},{30,94},{31,95},{32... | collective-permute-start | bytes 1585160 | tf_op jit(solution)/shard_map/ppermute | solution.py:264
  6.9 0.1 fusion
  7.0 0.2 convert_reduce_fusion
  7.2 0.1 select_reduce_fusion
  7.3 0.8 pad_maximum_fusion.refs_4_
  8.2 0.1 shard_map.28
  8.3 2.9 %collective-permute-start.2 = (bf16[2064,128]{1,0:T(8,128)(2,1)}, bf16[2064,128]{1,0:T(8,128)(2,1)}, u32[]{:S(2)}, u32[]{:S(2)}) collective-permute-start(bf16[2064,128]{1,0:T(8,128)(2,1)} %pad_maximum_fusion.refs_4_), channel_id=1, source_target_pairs={{0,192},{13,205},{14,206},{15,207},{16,208},{17,209},{30,222},{31,... | collective-permute-start | bytes 1585160 | tf_op jit(solution)/shard_map/ppermute | solution.py:264
  11.2 0.7 collective-permute-start.7
  11.9 1.8 %collective-permute-done.refs_1_ = bf16[2064,128]{1,0:T(8,128)(2,1)} collective-permute-done((bf16[2064,128]{1,0:T(8,128)(2,1)}, bf16[2064,128]{1,0:T(8,128)(2,1)}, u32[]{:S(2)}, u32[]{:S(2)}) %collective-permute-start) | collective-permute-done | bytes 528416 | tf_op jit(solution)/shard_map/ppermute | solution.py:264
  13.7 4.9 %collective-permute-start.4 = (bf16[2064,128]{1,0:T(8,128)(2,1)}, bf16[2064,128]{1,0:T(8,128)(2,1)}, u32[]{:S(2)}, u32[]{:S(2)}) collective-permute-start(bf16[2064,128]{1,0:T(8,128)(2,1)} %pad_maximum_fusion.refs_4_), channel_id=1, source_target_pairs={{0,64},{13,77},{14,78},{15,79},{16,80},{17,81},{30,94},{31,95},{32... | collective-permute-start | bytes 1585160 | tf_op jit(solution)/shard_map/ppermute | solution.py:264
  18.6 1.5 %collective-permute-start.1 = (bf16[2064,128]{1,0:T(8,128)(2,1)}, bf16[2064,128]{1,0:T(8,128)(2,1)}, u32[]{:S(2)}, u32[]{:S(2)}) collective-permute-start(bf16[2064,128]{1,0:T(8,128)(2,1)} %collective-permute-done.refs_1_), channel_id=1, source_target_pairs={{9,73},{10,74},{11,75},{12,76},{26,90},{27,91},{28,92},{29,93},{43... | collective-permute-start | bytes 1585160 | tf_op jit(solution)/shard_map/ppermute | solution.py:264
  20.1 5.0 %collective-permute-start.3 = (bf16[2064,128]{1,0:T(8,128)(2,1)}, bf16[2064,128]{1,0:T(8,128)(2,1)}, u32[]{:S(2)}, u32[]{:S(2)}) collective-permute-start(bf16[2064,128]{1,0:T(8,128)(2,1)} %slice.25.refs_0_), channel_id=1, source_target_pairs={{0,192},{13,205},{14,206},{15,207},{16,208},{17,209},{30,222},{31,... | collective-permute-start | bytes 1585160 | tf_op jit(solution)/shard_map/ppermute | solution.py:264
  25.0 1.5 %collective-permute-start.5 = (bf16[2064,128]{1,0:T(8,128)(2,1)}, bf16[2064,128]{1,0:T(8,128)(2,1)}, u32[]{:S(2)}, u32[]{:S(2)}) collective-permute-start(bf16[2064,128]{1,0:T(8,128)(2,1)} %collective-permute-done.2.refs_7_), channel_id=1, source_target_pairs={{1,193},{2,194},{3,195},{4,196},{18,210},{19,211},{20,212},{21,213... | collective-permute-start | bytes 1585160 | tf_op jit(solution)/shard_map/ppermute | solution.py:264
  26.6 1.6 %collective-permute-start.11 = (bf16[4112,128]{1,0:T(8,128)(2,1)S(1)}, bf16[4112,128]{1,0:T(8,128)(2,1)}, u32[]{:S(2)}, u32[]{:S(2)}) collective-permute-start(bf16[4112,128]{1,0:T(8,128)(2,1)S(1)} %collective-permute-done.7.refs_2_.refs_5_), channel_id=1, source_target_pairs={{0,15},{1,0},{2,1},{3,2},{4,3},{5,4},{6,5},{7,6},{8,7},{9,8},{10,9... | collective-permute-start | bytes 3158024 | tf_op jit(solution)/shard_map/ppermute | solution.py:264
  28.2 1.3 %collective-permute-start.8 = (bf16[4112,128]{1,0:T(8,128)(2,1)S(1)}, bf16[4112,128]{1,0:T(8,128)(2,1)S(1)}, u32[]{:S(2)}, u32[]{:S(2)}) collective-permute-start(bf16[4112,128]{1,0:T(8,128)(2,1)S(1)} %collective-permute-done.7.refs_2_.refs_5_), channel_id=1, source_target_pairs={{0,256},{1,257},{2,258},{3,259},{4,260},{5,261},{6,262},{7,263},{8... | collective-permute-start | bytes 3158024 | tf_op jit(solution)/shard_map/ppermute | solution.py:264
  29.5 2.3 %collective-permute-done.3.refs_3_ = bf16[2064,128]{1,0:T(8,128)(2,1)} collective-permute-done((bf16[2064,128]{1,0:T(8,128)(2,1)}, bf16[2064,128]{1,0:T(8,128)(2,1)}, u32[]{:S(2)}, u32[]{:S(2)}) %collective-permute-start.3) | collective-permute-done | bytes 528416 | tf_op jit(solution)/shard_map/ppermute | solution.py:264
  31.9 1.9 %shard_map.29.refs_0_.refs_1_ = bf16[4112,128]{1,0:T(8,128)(2,1)S(1)} custom-call(s32[7]{0:T(128)S(1)} %stack.35.meta, bf16[2064,128]{1,0:T(8,128)(2,1)} %slice.25.refs_0_, bf16[2064,128]{1,0:T(8,128)(2,1)} %collective-permute-done.refs_1_, bf16[2064,128]{1,0:T(8,128)(2,1)} %collective-permute-done.1.refs_2_, ...), custom_call_target="tpu_custom_call" | custom-call | flops 11500000256 | tf_op jit(solution)/shard_map/pallas_call | solution.py:224
  33.7 13.7 %collective-permute-start.6 = (bf16[4112,128]{1,0:T(8,128)(2,1)S(1)}, bf16[4112,128]{1,0:T(8,128)(2,1)S(1)}, u32[]{:S(2)}, u32[]{:S(2)}) collective-permute-start(bf16[4112,128]{1,0:T(8,128)(2,1)S(1)} %shard_map.29.refs_0_.refs_1_), channel_id=1, source_target_pairs={{0,16},{1,17},{2,18},{3,19},{4,20},{5,21},{6,22},{7,23},{8,24},{9,... | collective-permute-start | bytes 3158024 | tf_op jit(solution)/shard_map/ppermute | solution.py:264
  47.4 1.9 %collective-permute-start.9 = (bf16[4112,128]{1,0:T(8,128)(2,1)S(1)}, bf16[4112,128]{1,0:T(8,128)(2,1)}, u32[]{:S(2)}, u32[]{:S(2)}) collective-permute-start(bf16[4112,128]{1,0:T(8,128)(2,1)S(1)} %shard_map.29.refs_0_.refs_1_), channel_id=1, source_target_pairs={{0,288},{1,289},{2,290},{3,291},{4,292},{5,293},{6,294},{7,295},{8... | collective-permute-start | bytes 3158024 | tf_op jit(solution)/shard_map/ppermute | solution.py:264
  49.4 1.7 %collective-permute-start.13 = (bf16[4112,128]{1,0:T(8,128)(2,1)}, bf16[4112,128]{1,0:T(8,128)(2,1)}, u32[]{:S(2)}, u32[]{:S(2)}) collective-permute-start(bf16[4112,128]{1,0:T(8,128)(2,1)} %collective-permute-done.11.refs_7_), channel_id=1, source_target_pairs={{0,15},{1,0},{2,1},{3,2},{4,3},{5,4},{6,5},{7,6},{8,7},{9,8},{10,9... | collective-permute-start | bytes 3158024 | tf_op jit(solution)/shard_map/ppermute | solution.py:264
  51.0 4.2 %collective-permute-done.8.refs_3_.refs_6_ = bf16[4112,128]{1,0:T(8,128)(2,1)S(1)} collective-permute-done((bf16[4112,128]{1,0:T(8,128)(2,1)S(1)}, bf16[4112,128]{1,0:T(8,128)(2,1)S(1)}, u32[]{:S(2)}, u32[]{:S(2)}) %collective-permute-start.8) | collective-permute-done | bytes 1052704 | tf_op jit(solution)/shard_map/ppermute | solution.py:264
  55.3 1.3 %collective-permute-start.12 = (bf16[4112,128]{1,0:T(8,128)(2,1)}, bf16[4112,128]{1,0:T(8,128)(2,1)}, u32[]{:S(2)}, u32[]{:S(2)}) collective-permute-start(bf16[4112,128]{1,0:T(8,128)(2,1)} %collective-permute-done.11.refs_7_), channel_id=1, source_target_pairs={{0,256},{1,257},{2,258},{3,259},{4,260},{5,261},{6,262},{7,263},{8... | collective-permute-start | bytes 3158024 | tf_op jit(solution)/shard_map/ppermute | solution.py:264
  56.6 5.2 %shard_map.30.refs_0_ = f32[16,128,128]{2,1,0:T(8,128)S(1)} custom-call(s32[128]{0:T(128)S(1)} %get-tuple-element.16.own_table, s32[32]{0:T(128)S(1)} %bitcast_select_fusion.cells, s32[7]{0:T(128)S(1)} %stack.35.meta, bf16[4096,128]{1,0:T(8,128)(2,1)S(1)} %bitcast.23, bf16[4112,128]{1,0:T(8,128)(2,1)S(1)} %shard_map.29.refs_0_.refs_1_, ...), custom_call_target="tpu_custom_call" | custom-call | flops 115000000 | tf_op jit(solution)/shard_map/pallas_call | solution.py:238
  61.8 1.0 copy-done.3
  62.8 12.7 %collective-permute-done.9.ref = bf16[4112,128]{1,0:T(8,128)(2,1)} collective-permute-done((bf16[4112,128]{1,0:T(8,128)(2,1)S(1)}, bf16[4112,128]{1,0:T(8,128)(2,1)}, u32[]{:S(2)}, u32[]{:S(2)}) %collective-permute-start.9) | collective-permute-done | bytes 1052704 | tf_op jit(solution)/shard_map/ppermute | solution.py:264
  75.5 2.7 %collective-permute-start.10 = (bf16[4112,128]{1,0:T(8,128)(2,1)}, bf16[4112,128]{1,0:T(8,128)(2,1)S(1)}, u32[]{:S(2)}, u32[]{:S(2)}) collective-permute-start(bf16[4112,128]{1,0:T(8,128)(2,1)} %shard_map.31.refs_3_), channel_id=1, source_target_pairs={{0,16},{1,17},{2,18},{3,19},{4,20},{5,21},{6,22},{7,23},{8,24},{9,... | collective-permute-start | bytes 3158024 | tf_op jit(solution)/shard_map/ppermute | solution.py:264
  78.2 1.3 %collective-permute-start.14 = (bf16[4112,128]{1,0:T(8,128)(2,1)}, bf16[4112,128]{1,0:T(8,128)(2,1)S(1)}, u32[]{:S(2)}, u32[]{:S(2)}) collective-permute-start(bf16[4112,128]{1,0:T(8,128)(2,1)} %collective-permute-done.13.refs_9_), channel_id=1, source_target_pairs={{0,256},{1,257},{2,258},{3,259},{4,260},{5,261},{6,262},{7,263},{8... | collective-permute-start | bytes 3158024 | tf_op jit(solution)/shard_map/ppermute | solution.py:264
  79.5 1.2 %collective-permute-done.10.refs_4_ = bf16[4112,128]{1,0:T(8,128)(2,1)S(1)} collective-permute-done((bf16[4112,128]{1,0:T(8,128)(2,1)}, bf16[4112,128]{1,0:T(8,128)(2,1)S(1)}, u32[]{:S(2)}, u32[]{:S(2)}) %collective-permute-start.10) | collective-permute-done | bytes 1052704 | tf_op jit(solution)/shard_map/ppermute | solution.py:264
  80.7 4.2 %shard_map.32.refs_0_ = f32[16,128,128]{2,1,0:T(8,128)S(1)} custom-call(s32[128]{0:T(128)S(1)} %get-tuple-element.16.own_table, s32[32]{0:T(128)S(1)} %bitcast_select_fusion.cells, s32[7]{0:T(128)S(1)} %stack.35.meta, bf16[4096,128]{1,0:T(8,128)(2,1)S(1)} %bitcast.24, f32[16,128,128]{2,1,0:T(8,128)} %copy-done.3, bf16[4112,128]{1,0:T(8,128)(2,1)} %copy-done.1, ...), custom_call_target="tpu_custom_call" | custom-call | flops 115000000 | tf_op jit(solution)/shard_map/pallas_call | solution.py:238
  84.9 9.1 %collective-permute-done.14.refs_10_ = bf16[4112,128]{1,0:T(8,128)(2,1)S(1)} collective-permute-done((bf16[4112,128]{1,0:T(8,128)(2,1)}, bf16[4112,128]{1,0:T(8,128)(2,1)S(1)}, u32[]{:S(2)}, u32[]{:S(2)}) %collective-permute-start.14) | collective-permute-done | bytes 1052704 | tf_op jit(solution)/shard_map/ppermute | solution.py:264
  94.0 4.8 %shard_map.33 = f32[16,128,128]{2,1,0:T(8,128)} custom-call(s32[128]{0:T(128)S(1)} %get-tuple-element.16.own_table, s32[32]{0:T(128)S(1)} %bitcast_select_fusion.cells, s32[7]{0:T(128)S(1)} %stack.35.meta, bf16[4096,128]{1,0:T(8,128)(2,1)S(1)} %bitcast.25, f32[16,128,128]{2,1,0:T(8,128)S(1)} %shard_map.32.refs_0_, bf16[4112,128]{1,0:T(8,128)(2,1)} %copy-done.1, ...), custom_call_target="tpu_custom_call" | custom-call | flops 115000000 | tf_op jit(solution)/shard_map/pallas_call | solution.py:238
  (26 shorter events, 0.2 us)
Async XLA Ops:
  0.0 6.8 %copy-start = (bf16[1,1,32,128,128]{4,3,2,1,0:T(8,128)(2,1)S(1)}, bf16[1,1,32,128,128]{4,3,2,1,0:T(8,128)(2,1)}, u32[]{:S(2)}) copy-start(bf16[1,1,32,128,128]{4,3,2,1,0:T(8,128)(2,1)} %param.2) | copy-start | bytes 3145732
  0.0 6.9 %copy-start.4 = (s32[1,1,2,32]{3,2,1,0:T(2,128)S(1)}, s32[1,1,2,32]{3,2,1,0:T(2,128)}, u32[]{:S(2)}) copy-start(s32[1,1,2,32]{3,2,1,0:T(2,128)} %param.3) | copy-start | bytes 772
  2.0 11.8 %collective-permute-start = (bf16[2064,128]{1,0:T(8,128)(2,1)}, bf16[2064,128]{1,0:T(8,128)(2,1)}, u32[]{:S(2)}, u32[]{:S(2)}) collective-permute-start(bf16[2064,128]{1,0:T(8,128)(2,1)} %slice.25.refs_0_), channel_id=1, source_target_pairs={{0,64},{13,77},{14,78},{15,79},{16,80},{17,81},{30,94},{31,95},{32... | collective-permute-start | bytes 1585160 | tf_op jit(solution)/shard_map/ppermute | solution.py:264
  8.3 11.8 %collective-permute-start.2 = (bf16[2064,128]{1,0:T(8,128)(2,1)}, bf16[2064,128]{1,0:T(8,128)(2,1)}, u32[]{:S(2)}, u32[]{:S(2)}) collective-permute-start(bf16[2064,128]{1,0:T(8,128)(2,1)} %pad_maximum_fusion.refs_4_), channel_id=1, source_target_pairs={{0,192},{13,205},{14,206},{15,207},{16,208},{17,209},{30,222},{31,... | collective-permute-start | bytes 1585160 | tf_op jit(solution)/shard_map/ppermute | solution.py:264
  11.2 15.4 %collective-permute-start.7 = (bf16[4112,128]{1,0:T(8,128)(2,1)S(1)}, bf16[4112,128]{1,0:T(8,128)(2,1)S(1)}, u32[]{:S(2)}, u32[]{:S(2)}) collective-permute-start(bf16[4112,128]{1,0:T(8,128)(2,1)S(1)} %shard_map.28), channel_id=1, source_target_pairs={{0,15},{1,0},{2,1},{3,2},{4,3},{5,4},{6,5},{7,6},{8,7},{9,8},{10,9... | collective-permute-start | bytes 3158024 | tf_op jit(solution)/shard_map/ppermute | solution.py:264
  13.7 15.8 %collective-permute-start.4 = (bf16[2064,128]{1,0:T(8,128)(2,1)}, bf16[2064,128]{1,0:T(8,128)(2,1)}, u32[]{:S(2)}, u32[]{:S(2)}) collective-permute-start(bf16[2064,128]{1,0:T(8,128)(2,1)} %pad_maximum_fusion.refs_4_), channel_id=1, source_target_pairs={{0,64},{13,77},{14,78},{15,79},{16,80},{17,81},{30,94},{31,95},{32... | collective-permute-start | bytes 1585160 | tf_op jit(solution)/shard_map/ppermute | solution.py:264
  18.6 9.6 %collective-permute-start.1 = (bf16[2064,128]{1,0:T(8,128)(2,1)}, bf16[2064,128]{1,0:T(8,128)(2,1)}, u32[]{:S(2)}, u32[]{:S(2)}) collective-permute-start(bf16[2064,128]{1,0:T(8,128)(2,1)} %collective-permute-done.refs_1_), channel_id=1, source_target_pairs={{9,73},{10,74},{11,75},{12,76},{26,90},{27,91},{28,92},{29,93},{43... | collective-permute-start | bytes 1585160 | tf_op jit(solution)/shard_map/ppermute | solution.py:264
  20.1 11.8 %collective-permute-start.3 = (bf16[2064,128]{1,0:T(8,128)(2,1)}, bf16[2064,128]{1,0:T(8,128)(2,1)}, u32[]{:S(2)}, u32[]{:S(2)}) collective-permute-start(bf16[2064,128]{1,0:T(8,128)(2,1)} %slice.25.refs_0_), channel_id=1, source_target_pairs={{0,192},{13,205},{14,206},{15,207},{16,208},{17,209},{30,222},{31,... | collective-permute-start | bytes 1585160 | tf_op jit(solution)/shard_map/ppermute | solution.py:264
  25.0 6.8 %collective-permute-start.5 = (bf16[2064,128]{1,0:T(8,128)(2,1)}, bf16[2064,128]{1,0:T(8,128)(2,1)}, u32[]{:S(2)}, u32[]{:S(2)}) collective-permute-start(bf16[2064,128]{1,0:T(8,128)(2,1)} %collective-permute-done.2.refs_7_), channel_id=1, source_target_pairs={{1,193},{2,194},{3,195},{4,196},{18,210},{19,211},{20,212},{21,213... | collective-permute-start | bytes 1585160 | tf_op jit(solution)/shard_map/ppermute | solution.py:264
  26.6 22.8 %collective-permute-start.11 = (bf16[4112,128]{1,0:T(8,128)(2,1)S(1)}, bf16[4112,128]{1,0:T(8,128)(2,1)}, u32[]{:S(2)}, u32[]{:S(2)}) collective-permute-start(bf16[4112,128]{1,0:T(8,128)(2,1)S(1)} %collective-permute-done.7.refs_2_.refs_5_), channel_id=1, source_target_pairs={{0,15},{1,0},{2,1},{3,2},{4,3},{5,4},{6,5},{7,6},{8,7},{9,8},{10,9... | collective-permute-start | bytes 3158024 | tf_op jit(solution)/shard_map/ppermute | solution.py:264
  28.2 27.0 %collective-permute-start.8 = (bf16[4112,128]{1,0:T(8,128)(2,1)S(1)}, bf16[4112,128]{1,0:T(8,128)(2,1)S(1)}, u32[]{:S(2)}, u32[]{:S(2)}) collective-permute-start(bf16[4112,128]{1,0:T(8,128)(2,1)S(1)} %collective-permute-done.7.refs_2_.refs_5_), channel_id=1, source_target_pairs={{0,256},{1,257},{2,258},{3,259},{4,260},{5,261},{6,262},{7,263},{8... | collective-permute-start | bytes 3158024 | tf_op jit(solution)/shard_map/ppermute | solution.py:264
  33.7 28.1 %copy-start.1 = (bf16[4112,128]{1,0:T(8,128)(2,1)}, bf16[4112,128]{1,0:T(8,128)(2,1)S(1)}, u32[]{:S(2)}) copy-start(bf16[4112,128]{1,0:T(8,128)(2,1)S(1)} %shard_map.29.refs_0_.refs_1_) | copy-start | bytes 3158020
  33.7 22.8 %collective-permute-start.6 = (bf16[4112,128]{1,0:T(8,128)(2,1)S(1)}, bf16[4112,128]{1,0:T(8,128)(2,1)S(1)}, u32[]{:S(2)}, u32[]{:S(2)}) collective-permute-start(bf16[4112,128]{1,0:T(8,128)(2,1)S(1)} %shard_map.29.refs_0_.refs_1_), channel_id=1, source_target_pairs={{0,16},{1,17},{2,18},{3,19},{4,20},{5,21},{6,22},{7,23},{8,24},{9,... | collective-permute-start | bytes 3158024 | tf_op jit(solution)/shard_map/ppermute | solution.py:264
  47.4 28.1 %collective-permute-start.9 = (bf16[4112,128]{1,0:T(8,128)(2,1)S(1)}, bf16[4112,128]{1,0:T(8,128)(2,1)}, u32[]{:S(2)}, u32[]{:S(2)}) collective-permute-start(bf16[4112,128]{1,0:T(8,128)(2,1)S(1)} %shard_map.29.refs_0_.refs_1_), channel_id=1, source_target_pairs={{0,288},{1,289},{2,290},{3,291},{4,292},{5,293},{6,294},{7,295},{8... | collective-permute-start | bytes 3158024 | tf_op jit(solution)/shard_map/ppermute | solution.py:264
  49.4 28.8 %collective-permute-start.13 = (bf16[4112,128]{1,0:T(8,128)(2,1)}, bf16[4112,128]{1,0:T(8,128)(2,1)}, u32[]{:S(2)}, u32[]{:S(2)}) collective-permute-start(bf16[4112,128]{1,0:T(8,128)(2,1)} %collective-permute-done.11.refs_7_), channel_id=1, source_target_pairs={{0,15},{1,0},{2,1},{3,2},{4,3},{5,4},{6,5},{7,6},{8,7},{9,8},{10,9... | collective-permute-start | bytes 3158024 | tf_op jit(solution)/shard_map/ppermute | solution.py:264
  55.3 24.3 %collective-permute-start.12 = (bf16[4112,128]{1,0:T(8,128)(2,1)}, bf16[4112,128]{1,0:T(8,128)(2,1)}, u32[]{:S(2)}, u32[]{:S(2)}) collective-permute-start(bf16[4112,128]{1,0:T(8,128)(2,1)} %collective-permute-done.11.refs_7_), channel_id=1, source_target_pairs={{0,256},{1,257},{2,258},{3,259},{4,260},{5,261},{6,262},{7,263},{8... | collective-permute-start | bytes 3158024 | tf_op jit(solution)/shard_map/ppermute | solution.py:264
  56.6 5.2 %copy-start.2 = (bf16[4112,128]{1,0:T(8,128)(2,1)}, bf16[4112,128]{1,0:T(8,128)(2,1)S(1)}, u32[]{:S(2)}) copy-start(bf16[4112,128]{1,0:T(8,128)(2,1)S(1)} %collective-permute-done.6.refs_1_.refs_2_) | copy-start | bytes 3158020
  61.8 1.0 copy-start.3
  75.5 5.2 %collective-permute-start.10 = (bf16[4112,128]{1,0:T(8,128)(2,1)}, bf16[4112,128]{1,0:T(8,128)(2,1)S(1)}, u32[]{:S(2)}, u32[]{:S(2)}) collective-permute-start(bf16[4112,128]{1,0:T(8,128)(2,1)} %shard_map.31.refs_3_), channel_id=1, source_target_pairs={{0,16},{1,17},{2,18},{3,19},{4,20},{5,21},{6,22},{7,23},{8,24},{9,... | collective-permute-start | bytes 3158024 | tf_op jit(solution)/shard_map/ppermute | solution.py:264
  78.2 15.8 %collective-permute-start.14 = (bf16[4112,128]{1,0:T(8,128)(2,1)}, bf16[4112,128]{1,0:T(8,128)(2,1)S(1)}, u32[]{:S(2)}, u32[]{:S(2)}) collective-permute-start(bf16[4112,128]{1,0:T(8,128)(2,1)} %collective-permute-done.13.refs_9_), channel_id=1, source_target_pairs={{0,256},{1,257},{2,258},{3,259},{4,260},{5,261},{6,262},{7,263},{8... | collective-permute-start | bytes 3158024 | tf_op jit(solution)/shard_map/ppermute | solution.py:264
